TPU v7x, 256 devices: a whole 4x4x8 slice. The times are simulated.
256 devices in a mesh: pre: 8 (over y, core), wide: 32 (over x, z).
Axes of the slice: x: 4, y: 4, z: 8, core: 2. Of those that a mesh axis runs over, the one named last changes fastest.
Arguments:
- prompt_hidden: bfloat16 [16384, 8192], P('wide', 'pre'), may hold values from -6 to 6
- attn_gain: float32 [8192], replicated, may hold values from 0.25 to 1.75
- kv_weight: bfloat16 [8192, 2048], P(None, 'pre'), may hold values from -0.0625 to 0.0625
- prompt_lengths: int32 [512], P('wide'), may hold values from 1 to 32, as said below
- owner_slot: int32 [512], P('wide'), may hold values from 0 to 511, as said below
- new_queries: bfloat16 [1, 512, 8192], P(None, 'wide', 'pre'), may hold values from -60 to 60
- new_keys_values: bfloat16 [1, 512, 2048], P(None, 'wide', 'pre'), may hold values from -8 to 8
- out_weight: bfloat16 [8192, 8192], P('pre', 'wide'), may hold values from -0.0625 to 0.0625
- residual: bfloat16 [1, 512, 8192], P(None, None, 'wide'), may hold values from -6 to 6
- final_gain: float32 [8192], P('wide'), may hold values from 0.25 to 1.75
- vocab_weight: bfloat16 [8192, 65536], P('wide', 'pre'), may hold values from -3 to 3
- sampled_ids: int32 [1, 512], replicated, may hold values from 0 to 65535
Outputs:
- logprobs: float32 [1, 512], P(None, 'wide')
Inputs may be any that keep to these rules, and one draw needn't show every extreme that they name: `prompt_lengths`: some request has a prompt of exactly 32 positions. `owner_slot`: A permutation of the 512 decode rows; decode row o is owned by wide index o // 16. Each wide index owns 16 rows, and no two requests prefilled on one wide index go to the same owner.
All inputs are finite; a program needn't handle non-finite values.
Results may differ from a plain program's by a relative error of at most 0.003.
Values may be sent and summed in bfloat16 or wider, within the bound.
No kernel may reach another device: no remote copies, remote signals or barrier semaphores. Data moves between devices by JAX's collectives and lax.ppermute only.
A program may use at most 128 MiB of HBM per device.

v0:
```python
import jax
import jax.numpy as jnp
from jax import lax
from jax.sharding import PartitionSpec as P

D = 8192
HEAD_DIM = 128


epsilon = 1e-05
rope_base = 500000.0


def merged(value, axis, join):
    pieces = jax.tree.map(lambda part: lax.all_gather(part, axis), value)
    head = jax.tree.map(lambda part: part[0], pieces)
    tail = jax.tree.map(lambda part: part[1:], pieces)
    running, _ = lax.scan(lambda running, slab: (join(running, slab), None), head, tail)
    return running


def rotate(values_in, positions):
    half_dim = values_in.shape[-1] // 2
    frequency = rope_base ** (-jnp.arange(half_dim, dtype=jnp.float32) / half_dim)
    angles = positions[..., None] * frequency
    cosine = jnp.cos(angles)
    sine_part = jnp.sin(angles)
    first_half = values_in[..., :half_dim]
    second_half = values_in[..., half_dim:]
    return jnp.concatenate(
        [
            first_half * cosine - second_half * sine_part,
            second_half * cosine + first_half * sine_part,
        ],
        axis=-1,
    )


def attend(queries, new_pairs, cache_keys, cache_values, lengths):
    num_steps = queries.shape[0]
    cache_len = cache_keys.shape[1]
    positions = (lengths[None, :] + jnp.arange(num_steps, dtype=jnp.int32)[:, None]).astype(
        jnp.float32
    )
    rotated = rotate(queries.astype(jnp.float32), positions[:, :, None, None])
    new_keys = rotate(new_pairs[:, :, :, 0].astype(jnp.float32), positions[:, :, None])
    new_values = new_pairs[:, :, :, 1].astype(jnp.float32)
    factor = queries.shape[-1] ** (-0.5)
    cache_scores = jnp.einsum("srkgd,rckd->srkgc", rotated, cache_keys.astype(jnp.float32)) * factor
    live = jnp.arange(cache_len, dtype=jnp.int32)[None, :] < lengths[:, None]
    cache_scores = jnp.where(live[None, :, None, None, :], cache_scores, -1e30)
    own_scores = jnp.einsum("srkgd,urkd->srkgu", rotated, new_keys) * factor
    causal = jnp.arange(num_steps)[None, :] <= jnp.arange(num_steps)[:, None]
    own_scores = jnp.where(causal[:, None, None, None, :], own_scores, -1e30)
    scores = jnp.concatenate([cache_scores, own_scores], axis=-1)
    row_max = jnp.max(scores, axis=-1, keepdims=True)
    weights = jnp.exp(scores - row_max)
    weights = (weights / jnp.sum(weights, axis=-1, keepdims=True)).astype(jnp.bfloat16)
    mixed = jnp.einsum(
        "srkgc,rckd->srkgd",
        weights[..., :cache_len].astype(jnp.float32),
        cache_values.astype(jnp.float32),
    )
    mixed = mixed + jnp.einsum(
        "srkgu,urkd->srkgd", weights[..., cache_len:].astype(jnp.float32), new_values
    )
    return mixed.astype(jnp.bfloat16)


def summarize(logits, row_ids, first_column):
    highest = jnp.max(logits, axis=-1)
    summed_exp = jnp.sum(jnp.exp(logits - highest[:, None]), axis=-1)
    columns = first_column + jnp.arange(logits.shape[1], dtype=jnp.int32)
    target_logit = jnp.sum(jnp.where(columns[None, :] == row_ids[:, None], logits, 0.0), axis=-1)
    return (highest, summed_exp, target_logit)


def combine(earlier, later):
    highest = jnp.maximum(earlier[0], later[0])
    summed_exp = earlier[1] * jnp.exp(earlier[0] - highest) + later[1] * jnp.exp(later[0] - highest)
    return (highest, summed_exp, earlier[2] + later[2])


def local(
    prompt_hidden,
    attn_gain,
    kv_weight,
    prompt_lengths,
    owner_slot,
    new_queries,
    new_keys_values,
    out_weight,
    residual,
    final_gain,
    vocab_weight,
    sampled_ids,
):
    wide_count = lax.axis_size("wide")
    req_local = prompt_lengths.shape[0]
    cache_len = prompt_hidden.shape[0] // req_local
    kv_local = kv_weight.shape[1] // (2 * HEAD_DIM)
    num_steps = new_queries.shape[0]
    group_size = new_queries.shape[2] // (kv_local * HEAD_DIM)
    total_req = req_local * wide_count
    gathered = lax.all_gather(prompt_hidden, "pre", axis=1, tiled=True)
    hidden_wide = gathered.astype(jnp.float32)
    norm_factor = lax.rsqrt(jnp.mean(hidden_wide * hidden_wide, axis=-1, keepdims=True) + epsilon)
    normed = (hidden_wide * norm_factor * attn_gain).astype(jnp.bfloat16)
    projected = jnp.dot(normed, kv_weight, preferred_element_type=jnp.float32)
    projected = projected.reshape(req_local, cache_len, kv_local, 2, HEAD_DIM)
    cache_positions = jnp.arange(cache_len, dtype=jnp.int32).astype(jnp.float32)
    cache_keys = rotate(projected[:, :, :, 0], cache_positions[None, :, None]).astype(jnp.bfloat16)
    cache_values = projected[:, :, :, 1].astype(jnp.bfloat16)
    cache_rows = jnp.stack([cache_keys, cache_values], axis=3).reshape(req_local, -1)
    owners = owner_slot // req_local
    slots = owner_slot % req_local
    peer_index = jnp.arange(wide_count, dtype=jnp.int32)
    send_mask = owners[None, :] == peer_index[:, None]
    outgoing = jnp.dot(
        send_mask.astype(jnp.bfloat16), cache_rows, preferred_element_type=jnp.float32
    ).astype(jnp.bfloat16)
    outgoing = outgoing.reshape(wide_count, cache_len, kv_local * 2 * HEAD_DIM)
    send_lengths = jnp.sum(jnp.where(send_mask, prompt_lengths[None, :], 0), axis=1)
    send_slots = jnp.sum(jnp.where(send_mask, slots[None, :] + 1, 0), axis=1) - 1
    send_meta = jnp.stack([send_lengths, send_slots], axis=1)
    incoming, incoming_meta = (
        lax.all_to_all(outgoing, "wide", split_axis=0, concat_axis=0, tiled=True),
        lax.all_to_all(send_meta, "wide", split_axis=0, concat_axis=0, tiled=True),
    )
    place_mask = incoming_meta[:, 1][None, :] == jnp.arange(req_local, dtype=jnp.int32)[:, None]
    owned_cache = jnp.dot(
        place_mask.astype(jnp.bfloat16),
        incoming.reshape(wide_count, -1),
        preferred_element_type=jnp.float32,
    ).astype(jnp.bfloat16)
    owned_cache = owned_cache.reshape(req_local, cache_len, kv_local, 2, HEAD_DIM)
    owned_lengths = jnp.sum(jnp.where(place_mask, incoming_meta[:, 0][None, :], 0), axis=1)
    queries = new_queries.reshape(num_steps, req_local, kv_local, group_size, HEAD_DIM)
    new_pairs = new_keys_values.reshape(num_steps, req_local, kv_local, 2, HEAD_DIM)
    attended = attend(
        queries, new_pairs, owned_cache[:, :, :, 0], owned_cache[:, :, :, 1], owned_lengths
    )
    attended = attended.reshape(num_steps, req_local, -1)
    head_terms = jnp.einsum(
        "srh,hd->srd",
        lax.all_gather(attended, "wide", axis=1, tiled=True),
        out_weight,
        preferred_element_type=jnp.float32,
    )
    head_total = lax.psum(head_terms, "pre")
    updated = residual.astype(jnp.float32) + head_total
    square_part = jnp.sum(updated * updated, axis=-1)
    gained = (updated * final_gain).astype(jnp.bfloat16)
    gained_rows = jnp.transpose(gained, (1, 0, 2)).reshape(total_req * num_steps, -1)
    square_rows = jnp.transpose(square_part).reshape(-1)
    id_rows = jnp.transpose(sampled_ids).reshape(-1)
    vocab_local = vocab_weight.shape[1]
    own_rows = req_local * num_steps
    own_start = lax.axis_index("wide") * own_rows
    total_squares = lax.psum(square_rows, "wide")
    row_part = lax.psum_scatter(
        jnp.dot(gained_rows, vocab_weight, preferred_element_type=jnp.float32),
        "wide",
        scatter_dimension=0,
        tiled=True,
    )
    own_squares = lax.dynamic_slice_in_dim(total_squares, own_start, own_rows, 0)
    own_ids = lax.dynamic_slice_in_dim(id_rows, own_start, own_rows, 0)
    logits = row_part * lax.rsqrt(own_squares / D + epsilon)[:, None]
    row_stats = summarize(logits, own_ids, lax.axis_index("pre") * vocab_local)
    highest, summed_exp, target_logit = merged(row_stats, "pre", combine)
    logprob_rows = target_logit - highest - jnp.log(summed_exp)
    return jnp.transpose(logprob_rows.reshape(req_local, num_steps))


def solution(mesh):
    return jax.shard_map(
        local,
        mesh=mesh,
        in_specs=(
            P("wide", "pre"),
            P(),
            P(None, "pre"),
            P("wide"),
            P("wide"),
            P(None, "wide", "pre"),
            P(None, "wide", "pre"),
            P("pre", "wide"),
            P(None, None, "wide"),
            P("wide"),
            P("wide", "pre"),
            P(),
        ),
        out_specs=P(None, "wide"),
        check_vma=False,
    )
```

profile of v0, /device:TPU:1, one launch (start us, length us, event | category | flops | bytes accessed | tf_op | source)
XLA Modules:
  0.0 524.8 jit_solution(13457083520388644810)
XLA Ops:
  6.5 0.7 all-gather.6.cloned.1.call-update
  7.3 0.7 fusion.38
  7.9 0.7 select_reduce_fusion.3
  8.7 0.7 copy.94
  9.4 11.9 %all-to-all-start = ((s32[32,1,2]{2,1,0:T(1,128)}), s32[32,1,2]{2,1,0:T(1,128)S(1)}, u32[]{:S(2)}, u32[]{:S(2)}) async-start(s32[32,1,2]{2,1,0:T(1,128)} %copy.94), calls=%async_computation | async-start | bytes 32768 | tf_op jit(solution)/shard_map/all_to_all | solution.py:128
  21.2 0.7 reshape.549
  22.1 0.8 convert_bitcast_fusion
  22.9 7.0 %all-to-all-done = s32[32,1,2]{2,1,0:T(1,128)S(1)} async-done(((s32[32,1,2]{2,1,0:T(1,128)}), s32[32,1,2]{2,1,0:T(1,128)S(1)}, u32[]{:S(2)}, u32[]{:S(2)}) %all-to-all-start) | async-done | bytes 288 | tf_op jit(solution)/shard_map/all_to_all | solution.py:128
  30.1 35.7 %all-gather.6.cloned.1.call-done = bf16[512,8192]{1,0:T(8,128)(2,1)} async-done(((bf16[512,1024]{1,0:T(8,128)(2,1)}), bf16[512,8192]{1,0:T(8,128)(2,1)}) %all-gather.6.cloned.1.call-update) | async-done | bytes 8388624 | tf_op jit(solution)/shard_map/all_gather | solution.py:105
  65.8 5.3 %fusion.7 = f32[512]{0:T(512)S(1)} fusion(bf16[512,8192]{1,0:T(8,128)(2,1)} %all-gather.6.cloned.1.call-done), kind=kLoop, calls=%fused_computation.12 | loop fusion | flops 12582400 | bytes 8390656 | tf_op jit(solution)/shard_map/reduce_sum | solution.py:107
  71.0 0.5 copy-done.1
  71.5 4.7 fusion.10
  76.2 0.3 reshape.541
  76.5 0.2 slice.95
  76.7 0.3 slice.98
  77.3 0.3 copy.98
  77.6 0.2 reshape.542
  77.8 0.4 convolution_convert_fusion
  78.2 0.9 copy.116
  79.1 9.5 %all-to-all-start.1 = ((bf16[32,32,256]{2,1,0:T(8,128)(2,1)}), bf16[32,32,256]{2,1,0:T(8,128)(2,1)S(1)}, u32[]{:S(2)}, u32[]{:S(2)}) async-start(bf16[32,32,256]{2,1,0:T(8,128)(2,1)} %bitcast.43), calls=%async_computation.1 | async-start | bytes 1048576 | tf_op jit(solution)/shard_map/all_to_all | solution.py:127
  89.1 0.2 fusion.27
  89.3 13.3 %all-to-all-done.1 = bf16[32,32,256]{2,1,0:T(8,128)(2,1)S(1)} async-done(((bf16[32,32,256]{2,1,0:T(8,128)(2,1)}), bf16[32,32,256]{2,1,0:T(8,128)(2,1)S(1)}, u32[]{:S(2)}, u32[]{:S(2)}) %all-to-all-start.1) | async-done | bytes 524320 | tf_op jit(solution)/shard_map/all_to_all | solution.py:127
  102.6 0.3 copy.117
  102.9 0.2 convolution_convert_fusion.1
  103.1 0.2 reshape.545
  103.3 0.6 fusion.45
  103.9 0.2 fusion.24
  104.8 0.1 fusion.15
  105.0 0.6 reshape.554
  105.7 70.9 %all-gather.8.cloned.1.call-done = bf16[1,512,1024]{2,1,0:T(8,128)(2,1)} async-done(((bf16[1,16,1024]{2,1,0:T(8,128)(2,1)}), bf16[1,512,1024]{2,1,0:T(8,128)(2,1)}) %all-gather.8.cloned.1.call-update) | async-done | bytes 1048592 | tf_op jit(solution)/shard_map/all_gather | solution.py:146
  176.6 2.5 convolution_bitcast_fusion
  179.1 0.2 reduce-scatter.2.cloned.1.call-start
  179.4 65.8 %all-reduce.6.cloned.1.call-done = f32[1,512,256]{2,1,0:T(8,128)} async-done(((f32[1,512,256]{2,1,0:T(8,128)}), f32[1,512,256]{2,1,0:T(8,128)}) %all-reduce.6.cloned.1.call-update) | async-done | bytes 524304 | tf_op jit(solution)/shard_map/psum | solution.py:150
  245.2 10.4 %fusion.18 = f32[512,8192]{1,0:T(8,128)} fusion(bf16[256,8192]{1,0:T(8,128)(2,1)} %param.24, f32[1,512,256]{2,1,0:T(8,128)} %all-reduce.6.cloned.1.call-done, bf16[1,512,256]{2,1,0:T(8,128)(2,1)S(1)} %copy-done.3, f32[256]{0:T(256)S(1)} %copy-done.4), kind=kOutput, calls=%fused_computation.32 | convolution fusion | flops 2148007936 | bytes 21758976 | tf_op jit(solution)/shard_map/dot_general | solution.py:162
  255.6 0.6 copy-done.6
  256.3 0.6 dynamic-slice.1
  257.4 0.7 dynamic-slice_bitcast_fusion
  258.2 0.1 multiply_reduce_fusion
  258.3 61.4 %psum.15 = f32[512]{0:T(512)S(1)} all-reduce(f32[512]{0:T(512)S(1)} %multiply_reduce_fusion), channel_id=1, replica_groups=mesh['pre'=8,'wide'=32] {'wide'}, use_global_device_ids=true, to_apply=%region_9.10 | all-reduce | flops 512 | bytes 4096 | tf_op jit(solution)/shard_map/psum | solution.py:160
  319.8 177.3 %reduce-scatter.2.cloned.1.call-done = f32[16,8192]{1,0:T(8,128)} async-done(((f32[512,8192]{1,0:T(8,128)}), f32[16,8192]{1,0:T(8,128)}) %reduce-scatter.2.cloned.1.call-update) | async-done | bytes 524304 | tf_op jit(solution)/shard_map/reduce_scatter | solution.py:161
  497.1 1.3 multiply_reduce_fusion.1
  498.4 0.2 dynamic-update-slice
  498.7 1.4 select_reduce_fusion
  500.0 0.2 dynamic-update-slice.2
  500.3 0.2 dynamic-update-slice.1
  500.5 16.5 %all-reduce.3 = (f32[128]{0:T(128)S(1)}, f32[128]{0:T(128)S(1)}, f32[128]{0:T(128)S(1)}) all-reduce(f32[128]{0:T(128)S(1)} %dynamic-update-slice, f32[128]{0:T(128)S(1)} %dynamic-update-slice.1, f32[128]{0:T(128)S(1)} %dynamic-update-slice.2), channel_id=2, replica_groups=mesh['pre'=8,'wide'=32] {'pre'}, use_global_device_ids=true, to_apply=%add | all-reduce | flops 384 | bytes 3072
  517.4 0.3 while.14
  517.7 0.5 subtract_bitcast_fusion
  (70 shorter events, 2.7 us)
Async XLA Ops:
  6.5 170.1 %copy-start = (bf16[1024,256]{1,0:T(8,128)(2,1)S(1)}, bf16[1024,256]{1,0:T(8,128)(2,1)}, u32[]{:S(2)}) copy-start(bf16[1024,256]{1,0:T(8,128)(2,1)} %param.21) | copy-start | bytes 1572868
  6.5 64.5 %copy-start.5 = (f32[8192]{0:T(1024)S(1)}, f32[8192]{0:T(1024)}, u32[]{:S(2)}) copy-start(f32[8192]{0:T(1024)} %param.15) | copy-start | bytes 98308
  6.5 59.2 %all-gather.6.cloned.1.call-start = ((), (), s32[]{:S(2)}) async-start(), calls=%async_computation.3 | async-start | bytes 9437184 | tf_op jit(solution)/shard_map/all_gather | solution.py:105
  9.4 20.5 %all-to-all-start = ((s32[32,1,2]{2,1,0:T(1,128)}), s32[32,1,2]{2,1,0:T(1,128)S(1)}, u32[]{:S(2)}, u32[]{:S(2)}) async-start(s32[32,1,2]{2,1,0:T(1,128)} %copy.94), calls=%async_computation | async-start | bytes 32768 | tf_op jit(solution)/shard_map/all_to_all | solution.py:128
  65.8 5.8 %copy-start.1 = (bf16[512,8192]{1,0:T(8,128)(2,1)S(1)}, bf16[512,8192]{1,0:T(8,128)(2,1)}, u32[]{:S(2)}) copy-start(bf16[512,8192]{1,0:T(8,128)(2,1)} %all-gather.6.cloned.1.call-done) | copy-start | bytes 25165828
  76.2 169.0 %copy-start.3 = (bf16[1,512,256]{2,1,0:T(8,128)(2,1)S(1)}, bf16[1,512,256]{2,1,0:T(8,128)(2,1)}, u32[]{:S(2)}) copy-start(bf16[1,512,256]{2,1,0:T(8,128)(2,1)} %param.22) | copy-start | bytes 786436
  76.2 169.0 %copy-start.4 = (f32[256]{0:T(256)S(1)}, f32[256]{0:T(256)}, u32[]{:S(2)}) copy-start(f32[256]{0:T(256)} %param.23) | copy-start | bytes 3076
  79.1 23.5 %all-to-all-start.1 = ((bf16[32,32,256]{2,1,0:T(8,128)(2,1)}), bf16[32,32,256]{2,1,0:T(8,128)(2,1)S(1)}, u32[]{:S(2)}, u32[]{:S(2)}) async-start(bf16[32,32,256]{2,1,0:T(8,128)(2,1)} %bitcast.43), calls=%async_computation.1 | async-start | bytes 1048576 | tf_op jit(solution)/shard_map/all_to_all | solution.py:127
  88.6 88.0 %all-gather.8.cloned.1.call-start = ((), (), s32[]{:S(2)}) async-start(), calls=%async_computation.4 | async-start | bytes 1081344 | tf_op jit(solution)/shard_map/all_gather | solution.py:146
  105.6 139.5 %all-reduce.6.cloned.1.call-start = ((), (), s32[]{:S(2)}) async-start(), calls=%async_computation.5 | async-start | bytes 1048576 | tf_op jit(solution)/shard_map/psum | solution.py:150
  179.1 318.0 %reduce-scatter.2.cloned.1.call-start = ((), (), s32[]{:S(2)}) async-start(), calls=%async_computation.6 | async-start | bytes 17301504 | tf_op jit(solution)/shard_map/reduce_scatter | solution.py:161
  255.6 0.7 copy-start.6
  255.6 2.6 copy-start.2
Sparse Core Ops, SparseCore 0:
  9.2 56.5 all-gather.5
  105.8 70.8 all-gather.7
  179.3 65.8 all-reduce.5
  255.8 241.3 reduce-scatter.1
where the time goes:
time: 525 us
  waiting for transfers between devices  371 us (71%)
  blocking collectives  77.9 us (15%)
  starting transfers between devices  21.7 us (4%)
  matrix products  18.8 us (4%)
  between operations  14 us (3%)
  other arithmetic  12.2 us (2%)
  local copies, waits for them, and re-layouts  9.45 us (2%)
    reduce_scatter x1, waiting for transfers between devices, local(): lax.psum_scatter(jnp.dot(gained_rows, vocab_weight, preferred_element_typ...  177 us
    all_gather x1, waiting for transfers between devices, local(): lax.all_gather(attended, 'wide', axis=1, tiled=True)  70.9 us
    psum x1, waiting for transfers between devices, local(): head_total = lax.psum(head_terms, 'pre')  65.8 us
    psum x1, blocking collectives, local(): total_squares = lax.psum(square_rows, 'wide')  61.4 us
    all_gather x1, waiting for transfers between devices, local(): gathered = lax.all_gather(prompt_hidden, 'pre', axis=1, tiled=True)  35.7 us
    unnamed x1, blocking collectives  16.5 us
    all_to_all x1, waiting for transfers between devices, local(): lax.all_to_all(outgoing, 'wide', split_axis=0, concat_axis=0, tiled=True)  13.3 us
    all_to_all x1, starting transfers between devices, local(): lax.all_to_all(send_meta, 'wide', split_axis=0, concat_axis=0, tiled=True)  11.9 us
  transfers between devices with their start and end apart: 6, of which 6 were waited for; matrix products, arithmetic and copies ran while one was open for 1% of the time, Pallas kernels for 0%

commit v1 on v0

v1 whole, which is shorter than its diff:
```python
import functools

import jax
import jax.numpy as jnp
import numpy as np
from jax import lax
from jax.experimental import pallas as pl
from jax.experimental.pallas import tpu as pltpu
from jax.sharding import Mesh, PartitionSpec as P

HEAD_DIM = 128
LANES = 128
CORES = 2
X = 4
LOW = 2

epsilon = 1e-05
rope_base = 500000.0

f32 = jnp.float32
bf16 = jnp.bfloat16


def rope_turns(positions, xp=jnp):
    half_dim = HEAD_DIM // 2
    frequency = rope_base ** (-np.arange(half_dim) / half_dim)
    angles = positions.astype(f32)[:, None] * frequency.astype(np.float32)
    cosine = xp.cos(angles)
    sine = xp.sin(angles)
    return xp.stack(
        [
            xp.concatenate([cosine, cosine], axis=1),
            xp.concatenate([-sine, sine], axis=1),
        ]
    )


def shift(value, axis, step):
    count = lax.axis_size(axis)
    return lax.ppermute(value, axis, [(i, (i + step) % count) for i in range(count)])


def swap(value):
    return shift(value, "c", 1)


def rows_at(value, start, count):
    return lax.dynamic_slice_in_dim(value, start, count, 0)


def in_three(value):
    high = lax.reduce_precision(value, 8, 7)
    rest = value - high
    middle = lax.reduce_precision(rest, 8, 7)
    return high.astype(bf16), middle.astype(bf16), (rest - middle).astype(bf16)


def dot(a, b):
    return jnp.dot(a, b, preferred_element_type=f32)


def dot_t(a, b):
    return lax.dot_general(a, b, (((1,), (1,)), ((), ())), preferred_element_type=f32)


def attend_kernel(
    width,
    cache_len,
    hidden_ref,
    weight_ref,
    gain_ref,
    key_turns_ref,
    picked_ref,
    turns_ref,
    lengths_ref,
    out_ref,
    sums_ref,
    squares_ref,
):
    step = pl.program_id(0)
    wide = hidden_ref[0].astype(f32)
    squares = jnp.sum(wide * wide, axis=1, keepdims=True)
    sums = dot((wide * gain_ref[0]).astype(bf16), weight_ref[...])

    @pl.when(step == 0)
    def _():
        sums_ref[...] = sums
        squares_ref[...] = squares

    @pl.when(step > 0)
    def _():
        sums_ref[...] += sums
        squares_ref[...] += squares

    @pl.when(step == pl.num_programs(0) - 1)
    def _():
        norm_factor = lax.rsqrt(squares_ref[...] * (1.0 / width) + epsilon)
        projected = sums_ref[...] * norm_factor
        requests = lengths_ref.shape[0]
        tokens = projected.shape[0]
        picked = picked_ref[...].astype(f32)
        groups = picked.shape[1] // HEAD_DIM - 2
        factor = HEAD_DIM ** (-0.5)

        def turned(rows, turns):
            return rows * turns[0] + pltpu.roll(rows, HEAD_DIM // 2, 1) * turns[1]

        columns = [picked[:, g * HEAD_DIM : (g + 1) * HEAD_DIM] for g in range(groups + 2)]
        queries = [turned(rows, turns_ref) for rows in columns[:groups]]
        new_key = turned(columns[groups], turns_ref)
        own = [jnp.sum(rows * new_key, axis=1, keepdims=True) * factor for rows in queries]
        own = jnp.concatenate(own, axis=0)
        queries = jnp.concatenate(queries, axis=0)
        new_values = jnp.concatenate([columns[groups + 1]] * groups, axis=0)
        token = lax.broadcasted_iota(jnp.int32, (requests, tokens), 1)
        request = lax.broadcasted_iota(jnp.int32, (requests, tokens), 0)
        start = request * cache_len
        live = (token >= start) & (token < start + lengths_ref[...])
        bias = jnp.where(live, 0.0, -1e30)
        bias = jnp.concatenate([bias] * groups, axis=0)
        keys = turned(projected[:, :HEAD_DIM], key_turns_ref).astype(bf16)
        values = projected[:, HEAD_DIM:].astype(bf16)
        upper = queries.astype(bf16)
        lower = (queries - upper.astype(f32)).astype(bf16)
        scores = (dot_t(upper, keys) + dot_t(lower, keys)) * factor + bias
        row_max = jnp.maximum(jnp.max(scores, axis=1, keepdims=True), own)
        weights = jnp.exp(scores - row_max)
        own_weight = jnp.exp(own - row_max)
        total = jnp.sum(weights, axis=1, keepdims=True) + own_weight
        weights = (weights / total).astype(bf16)
        own_weight = (own_weight / total).astype(bf16).astype(f32)
        mixed = dot(weights, values) + own_weight * new_values
        pieces = [mixed[g * requests : (g + 1) * requests] for g in range(groups)]
        mixed = jnp.concatenate(pieces, axis=1).astype(bf16)
        out_ref[...] = jnp.broadcast_to(mixed[None], out_ref.shape)


def three_columns(value):
    column = lax.broadcasted_iota(jnp.int32, (value.shape[0], LANES), 1)
    terms = jnp.zeros((value.shape[0], LANES), f32)
    for place, term in enumerate(in_three(value)):
        terms = jnp.where(column == place, term.astype(f32), terms)
    return terms.astype(bf16)


def logits_kernel(decode_shape, place_ref, gains_ref, order_ref, *refs):
    outs = decode_shape[0]
    held = (len(refs) - outs) // 2
    from_refs, out_refs = refs[:held], refs[held : held + outs]
    held_refs, sems = refs[held + outs : -1], refs[-1]
    copies = [
        pltpu.make_async_copy(from_ref, held_ref, sems.at[index])
        for index, (from_ref, held_ref) in enumerate(zip(from_refs, held_refs))
    ]
    for copy in copies:
        copy.start()
    weight_refs = held_refs[2:]
    depth, out_cols = weight_refs[0].shape
    parts = held_refs[0].shape[0]
    lows = len(weight_refs) // parts
    inverse = [1.0 / gains_ref[index] for index in range(parts)]
    squares = []
    for copy, rows_ref in zip(copies[:2], held_refs[:2]):
        copy.wait()
        total = jnp.zeros(rows_ref.shape[1:], f32)
        for index in range(parts):
            updated = rows_ref[index].astype(f32) * inverse[index]
            total = total + updated * updated
        squares.append(three_columns(jnp.sum(total, axis=1, keepdims=True)))
    totals = [None, None]
    for index, weight_ref in enumerate(weight_refs):
        place = lax.rem(place_ref[2] - index // lows + parts, parts)
        low = lax.rem(place_ref[1] + index % lows, lows)
        start = pl.multiple_of(low * depth, depth)
        copies[2 + index].wait()
        for half, rows_ref in enumerate(held_refs[:2]):
            term = dot(rows_ref[place, :, pl.ds(start, depth)], weight_ref[...])
            totals[half] = term if index == 0 else totals[half] + term
    high_count, x_count, low_count, requests = decode_shape
    rows = order_ref.shape[1]
    row = lax.broadcasted_iota(jnp.int32, (rows, rows), 0)
    within = row % (low_count * requests)
    x_place = row // (low_count * requests) % x_count
    high_place = (row // (low_count * requests * x_count) + place_ref[3]) % high_count
    decode_row = (x_place * high_count + high_place) * (low_count * requests) + within
    permutation = (decode_row == order_ref[...]).astype(f32).astype(bf16)
    logits = jnp.concatenate([total.astype(bf16) for total in totals], axis=0)
    logits = dot(permutation, logits).astype(bf16)
    squares = dot(permutation, jnp.concatenate(squares, axis=0)).astype(bf16)
    block = rows // outs
    for index, out_ref in enumerate(out_refs):
        out_ref[:, :out_cols] = logits[index * block : (index + 1) * block]
        out_ref[:, out_cols:] = squares[index * block : (index + 1) * block]


def project_kernel(place_ref, rows_ref, mine_ref, near_ref, kept_ref, given_ref):
    core = place_ref[0]
    low = place_ref[1]
    groups, requests, depth = rows_ref.shape
    rows = rows_ref[...].reshape(groups * requests, depth)
    mine = dot(rows, mine_ref[...])
    near = dot(rows, near_ref[...])
    terms = jnp.concatenate(
        [jnp.where(low == 0, mine, near), jnp.where(low == 0, near, mine)], axis=1
    )
    terms = terms.reshape(groups, CORES, requests // CORES, terms.shape[1])
    first, second = terms[:, 0], terms[:, 1]
    kept_ref[...] = jnp.where(core == 0, first, second)
    given_ref[...] = jnp.where(core == 0, second, first)


def local(
    prompt_hidden,
    attn_gain,
    kv_weight,
    prompt_lengths,
    owner_slot,
    new_queries,
    new_keys_values,
    out_weight,
    residual,
    final_gain,
    vocab_weight,
    sampled_ids,
):
    core = lax.axis_index("c")
    y = lax.axis_index("y")
    x = lax.axis_index("x")
    high = lax.axis_index("h")
    low = lax.axis_index("l")
    y_count = lax.axis_size("y")
    x_count = lax.axis_size("x")
    high_count = lax.axis_size("h")
    low_count = lax.axis_size("l")
    z_count = high_count * low_count
    wide = x_count * z_count
    z = high * low_count + low
    me = x * z_count + z
    wide_axes = ("x", "h", "l")

    width = attn_gain.shape[0]
    requests = prompt_lengths.shape[0]
    half = requests // CORES
    total_rows = requests * wide
    cache_len = prompt_hidden.shape[0] // requests
    tokens = prompt_hidden.shape[0]
    depth = prompt_hidden.shape[1]

    hidden = lax.all_gather(prompt_hidden, ("y", "c"), axis=0)

    columns = out_weight.shape[1]
    vocab_local = vocab_weight.shape[1]
    group = low_count * x_count
    vocab_cols = vocab_local // group

    def sent_block(vocab_weight, d, e):
        place = lax.rem(x + d, x_count) * low_count + lax.rem(low + e, low_count)
        return lax.dynamic_slice_in_dim(vocab_weight, place * vocab_cols, vocab_cols, 1)

    def moved(block, d, e):
        pairs = [
            (i * low_count + j, (i + d) % x_count * low_count + (j + e) % low_count)
            for i in range(x_count)
            for j in range(low_count)
        ]
        return lax.ppermute(block, ("x", "l"), pairs)

    first_places = [(1, 0), (3, 0)]
    vocab_blocks = {place: sent_block(vocab_weight, *place) for place in first_places}
    vocab_later, prompt_lengths = lax.optimization_barrier((vocab_weight, prompt_lengths))
    for d in range(x_count):
        for e in range(low_count):
            if (d, e) not in vocab_blocks:
                vocab_blocks[d, e] = sent_block(vocab_later, d, e)

    told = jnp.concatenate([owner_slot.astype(f32), final_gain])
    width_told = -(-told.shape[0] // LANES) * LANES
    told = jnp.pad(told, (0, width_told - told.shape[0]))
    told = lax.all_to_all(
        jnp.broadcast_to(told[None, None, :], (wide, 1, width_told)),
        wide_axes,
        0,
        0,
        tiled=True,
    )

    def phase(places, *others):
        done = {place: moved(vocab_blocks[place], *place) for place in places}
        done, others, waiting = lax.optimization_barrier(
            (done, others, {k: v for k, v in vocab_blocks.items() if k not in done})
        )
        vocab_blocks.update(done)
        vocab_blocks.update(waiting)
        return others

    told, out_near = phase(first_places, told, shift(out_weight, "l", 1))
    owners = told[:, :, :requests].astype(jnp.int32)

    decode_rows = jnp.concatenate([new_queries[0], new_keys_values[0]], axis=1)
    own_rows = me * requests + jnp.arange(requests, dtype=jnp.int32)
    wanted = jnp.any(owners == own_rows[None, :, None], axis=2).astype(bf16)
    outgoing = dot(wanted, decode_rows).astype(bf16)
    incoming = lax.all_to_all(outgoing[:, None, :], wide_axes, 0, 0, tiled=True)
    told, incoming = phase([(1, 1), (3, 1)], told, incoming)
    owners = told[:, :, :requests].astype(jnp.int32)
    gains = told[:, 0, requests : requests + columns]
    gains = gains.reshape(x_count, high_count, low_count * columns)
    gains = lax.dynamic_index_in_dim(gains, high, 1)
    incoming = incoming[:, 0]
    pick = (owner_slot // requests)[:, None] == jnp.arange(wide, dtype=jnp.int32)[None, :]
    picked = dot(pick.astype(bf16), incoming).astype(bf16)
    head_width = new_queries.shape[2]

    row_block = requests // CORES * high_count
    by_place = owners.reshape(x_count, high_count, low_count, CORES, half)
    here = lax.dynamic_index_in_dim(by_place, y, 0, keepdims=False)
    here = lax.dynamic_index_in_dim(here, core, 2, keepdims=False)
    decode_index = jnp.arange(total_rows, dtype=jnp.int32)

    def residual_rows(place):
        rows = lax.dynamic_index_in_dim(here, place, 1, keepdims=False).reshape(-1)
        pick = (rows[:, None] == decode_index[None, :]).astype(bf16)
        return dot(pick, residual[0]).astype(bf16)

    def of_pair(mine, near):
        return jnp.where(
            low == 0,
            jnp.concatenate([mine, near], axis=1),
            jnp.concatenate([near, mine], axis=1),
        )

    residual_here = of_pair(
        residual_rows(low), shift(residual_rows(1 - low), "l", 1)
    ).astype(f32)
    gain_here = lax.dynamic_index_in_dim(gains, x, 0, keepdims=False)

    blocks = hidden.shape[0]
    places = x_count * high_count
    kv_columns = kv_weight.shape[1]

    def whole(*shape):
        return pl.BlockSpec(shape, lambda step: (0,) * len(shape))

    attended = pl.pallas_call(
        functools.partial(attend_kernel, width, cache_len),
        grid=(blocks,),
        out_shape=jax.ShapeDtypeStruct((places, requests, head_width), bf16),
        in_specs=[
            pl.BlockSpec((1, tokens, depth), lambda step: (step, 0, 0)),
            pl.BlockSpec((depth, kv_columns), lambda step: (step, 0)),
            pl.BlockSpec((1, 1, depth), lambda step: (step, 0, 0)),
            whole(2, tokens, HEAD_DIM),
            whole(requests, head_width + kv_columns),
            whole(2, requests, HEAD_DIM),
            whole(requests, 1),
        ],
        out_specs=whole(places, requests, head_width),
        scratch_shapes=[pltpu.VMEM((tokens, kv_columns), f32), pltpu.VMEM((tokens, 1), f32)],
        compiler_params=pltpu.CompilerParams(vmem_limit_bytes=60 * 1024 * 1024),
    )(
        hidden,
        kv_weight,
        attn_gain.reshape(blocks, 1, depth),
        rope_turns(np.arange(tokens) % cache_len, np),
        picked,
        rope_turns(prompt_lengths),
        prompt_lengths[:, None],
    )

    (attended,) = phase([(2, 0), (2, 1), (0, 1)], attended)
    attended = lax.all_to_all(attended, ("x", "h"), 0, 0, tiled=True)
    place = jnp.stack([core, low, x, high]).astype(jnp.int32)
    smem = pl.BlockSpec(memory_space=pltpu.SMEM)
    vmem = pl.BlockSpec(memory_space=pltpu.VMEM)
    part = jax.ShapeDtypeStruct((places, half, low_count * columns), f32)
    kept, given = pl.pallas_call(
        project_kernel,
        out_shape=(part, part),
        in_specs=[smem, vmem, vmem, vmem],
        out_specs=(vmem, vmem),
        compiler_params=pltpu.CompilerParams(vmem_limit_bytes=24 * 1024 * 1024),
    )(place, attended, out_weight, out_near)
    terms = (kept + swap(given)).reshape(x_count * row_block, -1)
    updated = residual_here + rows_at(terms, y * row_block, row_block)
    for step in range(1, y_count):
        part = rows_at(terms, lax.rem(y + step, y_count) * row_block, row_block)
        updated = updated + shift(part, "y", step)
    gained = (updated * gain_here).astype(bf16)

    count = x_count * low_count * y_count
    gathered = lax.all_to_all(
        jnp.broadcast_to(gained[None], (count,) + gained.shape), ("x", "l", "y"), 0, 0, tiled=True
    )
    gathered = gathered.reshape(x_count, count // x_count * row_block, -1)

    request_order = jnp.transpose(by_place, (3, 2, 0, 1, 4))
    request_order = jnp.where(core == 0, request_order, request_order[::-1]).reshape(-1)
    weights = [vocab_blocks[d, e] for d in range(x_count) for e in range(low_count)]
    operands = [gathered, swap(gathered)] + weights
    part = jax.ShapeDtypeStruct((total_rows // high_count, vocab_cols + LANES), bf16)
    partial = pl.pallas_call(
        functools.partial(logits_kernel, (high_count, x_count, low_count, requests)),
        out_shape=(part,) * high_count,
        in_specs=[smem, vmem, vmem] + [pl.BlockSpec(memory_space=pl.ANY)] * len(operands),
        out_specs=(vmem,) * high_count,
        scratch_shapes=[pltpu.VMEM(value.shape, bf16) for value in operands]
        + [pltpu.SemaphoreType.DMA((len(operands),))],
        compiler_params=pltpu.CompilerParams(vmem_limit_bytes=60 * 1024 * 1024),
    )(place, gains, request_order[None, :], *operands)
    parts = [partial[0]] + [shift(partial[d], "h", d) for d in (2, 1, 3)]
    summed = sum(value.astype(f32) for value in parts)
    own_squares = jnp.sum(summed[:, vocab_cols : vocab_cols + 3], axis=1, keepdims=True)
    logits = summed[:, :vocab_cols] * lax.rsqrt(own_squares / width + epsilon)

    id_rows = sampled_ids.reshape(x_count, high_count, low_count, requests)
    id_rows = lax.dynamic_index_in_dim(id_rows, high, 1, keepdims=False).reshape(-1)
    first = (y * CORES + core) * vocab_local + (x * low_count + low) * vocab_cols
    column_ids = first + jnp.arange(vocab_cols, dtype=jnp.int32)
    highest = jnp.max(logits, axis=-1)
    summed_exp = jnp.sum(jnp.exp(logits - highest[:, None]), axis=-1)
    target = jnp.sum(jnp.where(column_ids[None, :] == id_rows[:, None], logits, 0.0), axis=-1)
    stats = jnp.stack([highest, summed_exp, target]).reshape(3, group, requests)
    stats = jnp.transpose(stats, (1, 0, 2)).reshape(group, 3 * requests)
    stats = jnp.pad(stats, ((0, 0), (0, LANES - 3 * requests)))
    ends = y_count * CORES
    stats = jnp.broadcast_to(stats[None], (ends, group, LANES)).reshape(ends * group, 1, LANES)
    stats = lax.all_to_all(stats, ("y", "c", "x", "l"), 0, 0, tiled=True)[:, 0]
    all_highest = stats[:, :requests]
    top = jnp.max(all_highest, axis=0)
    sum_all = jnp.sum(
        stats[:, requests : 2 * requests] * jnp.exp(all_highest - top[None, :]), axis=0
    )
    target_all = jnp.sum(stats[:, 2 * requests : 3 * requests], axis=0)
    return (target_all - top - jnp.log(sum_all))[None, :]


def solution(mesh):
    pre, wide = mesh.devices.shape
    shape = (pre // CORES, CORES, X, wide // X // LOW, LOW)
    fine = Mesh(mesh.devices.reshape(shape), ("y", "c", "x", "h", "l"))
    pre_axes = ("y", "c")
    wide_axes = ("x", "h", "l")
    return jax.shard_map(
        local,
        mesh=fine,
        in_specs=(
            P(wide_axes, pre_axes),
            P(),
            P(None, pre_axes),
            P(wide_axes),
            P(wide_axes),
            P(None, wide_axes, pre_axes),
            P(None, wide_axes, pre_axes),
            P(pre_axes, wide_axes),
            P(None, None, wide_axes),
            P(wide_axes),
            P(wide_axes, pre_axes),
            P(),
        ),
        out_specs=P(None, wide_axes),
        check_vma=False,
    )
```

time: 525 us -> 206 us (0.39)
  waiting for transfers between devices: 371 us -> 63.6 us
  blocking collectives: 77.9 us -> 32.2 us
  starting transfers between devices: 21.7 us -> 52.9 us
  Pallas kernels: 0 us -> 19 us
  matrix products: 18.8 us -> 3.07 us
    reduce_scatter x1 -> x0, waiting for transfers between devices: 177 us -> none  [local(): lax.psum_scatter(jnp.dot(gained_rows, vocab_weight, preferred_element_typ...]
    all_gather x2 -> x1, waiting for transfers between devices: 107 us -> 0.01 us  [local(): hidden = lax.all_gather(prompt_hidden, ('y', 'c'), axis=0)]
    psum x1 -> x0, waiting for transfers between devices: 65.8 us -> none  [local(): head_total = lax.psum(head_terms, 'pre')]
    psum x1 -> x0, blocking collectives: 61.4 us -> none  [local(): total_squares = lax.psum(square_rows, 'wide')]
    ppermute x0 -> x17, starting transfers between devices: none -> 34.4 us  [the longest x10 23 us: shift(): lax.ppermute(value, axis, [(i, (i + step) % count) for i in range(count)])]
    all_to_all x0 -> x2, blocking collectives: none -> 32.2 us  [the longest x1 18.6 us: local(): lax.all_to_all(jnp.broadcast_to(gained[None], (count,) + gained.shape), (...]
    ppermute x0 -> x17, waiting for transfers between devices: none -> 30.8 us  [the longest x10 27.6 us: shift(): lax.ppermute(value, axis, [(i, (i + step) % count) for i in range(count)])]
    pallas_call x0 -> x3, Pallas kernels: none -> 19 us  [the longest x1 10.8 us: local(): pl.pallas_call(functools.partial(attend_kernel, width, cache_len), grid=(...]
  transfers between devices with their start and end apart: 6 -> 21, of which waited for: 6 -> 10; matrix products, arithmetic and copies ran while one was open for 1% -> 10% of each run, Pallas kernels for 0% -> 5%
where the time goes in v1:
time: 206 us
  waiting for transfers between devices  63.6 us (31%)
  starting transfers between devices  52.9 us (26%)
  blocking collectives  32.2 us (16%)
  Pallas kernels  19 us (9%)
  between operations  13.9 us (7%)
  local copies, waits for them, and re-layouts  13.3 us (6%)
  other arithmetic  7.54 us (4%)
  matrix products  3.07 us (1%)
    ppermute x10, waiting for transfers between devices, shift(): lax.ppermute(value, axis, [(i, (i + step) % count) for i in range(count)])  27.6 us
    ppermute x10, starting transfers between devices, shift(): lax.ppermute(value, axis, [(i, (i + step) % count) for i in range(count)])  23 us
    all_to_all x1, blocking collectives, local(): lax.all_to_all(jnp.broadcast_to(gained[None], (count,) + gained.shape), (...  18.6 us
    all_to_all x1, waiting for transfers between devices, local(): incoming = lax.all_to_all(outgoing[:, None, :], wide_axes, 0, 0, tiled=True)  14.1 us
    all_to_all x1, blocking collectives, local(): stats = lax.all_to_all(stats, ('y', 'c', 'x', 'l'), 0, 0, tiled=True)[:, 0]  13.6 us
    all_to_all x1, waiting for transfers between devices, local(): attended = lax.all_to_all(attended, ('x', 'h'), 0, 0, tiled=True)  13.1 us
    ppermute x7, starting transfers between devices, moved(): return lax.ppermute(block, ('x', 'l'), pairs)  11.4 us
    pallas_call x1, Pallas kernels, local(): pl.pallas_call(functools.partial(attend_kernel, width, cache_len), grid=(...  10.8 us
  transfers between devices with their start and end apart: 21, of which 10 were waited for; matrix products, arithmetic and copies ran while one was open for 10% of the time, Pallas kernels for 5%

profile of v1, /device:TPU:1, one launch (start us, length us, event | category | flops | bytes accessed | tf_op | source)
XLA Modules:
  0.0 205.5 jit_solution(393515771889550098)
XLA Ops:
  6.5 0.7 all-gather.3.cloned.1.call-update
  7.3 1.3 constant_dynamic-slice_fusion.14
  8.6 2.1 %collective-permute-start = (bf16[256,1024]{1,0:T(8,128)(2,1)S(1)}, bf16[256,1024]{1,0:T(8,128)(2,1)S(1)}, u32[]{:S(2)}, u32[]{:S(2)}) collective-permute-start(bf16[256,1024]{1,0:T(8,128)(2,1)S(1)} %get-tuple-element.92), channel_id=1, source_target_pairs={{0,8},{1,9},{8,16},{9,17},{16,24},{17,25},{24,0},{25,1},{2,10},{3,... | collective-permute-start | bytes 1572872 | tf_op jit(solution)/shard_map/ppermute | solution.py:266
  10.7 1.4 collective-permute-start.1
  12.1 1.7 collective-permute-start.2
  13.8 0.7 and_select_fusion
  14.5 0.8 select_maximum_fusion
  15.9 8.9 %all-to-all-start = ((f32[32,1,384]{2,1,0:T(1,128)}), f32[32,1,384]{2,1,0:T(1,128)S(1)}, u32[]{:S(2)}, u32[]{:S(2)}) async-start(f32[32,1,384]{2,1,0:T(1,128)} %broadcast_in_dim.13), calls=%async_computation | async-start | bytes 98304 | tf_op jit(solution)/shard_map/all_to_all | solution.py:279
  24.9 3.8 %constant_dynamic-slice_fusion.8 = (bf16[256,1024]{1,0:T(8,128)(2,1)S(1)}, bf16[256,1024]{1,0:T(8,128)(2,1)}, bf16[256,1024]{1,0:T(8,128)(2,1)}, bf16[256,1024]{...) fusion(bf16[256,8192]{1,0:T(8,128)(2,1)} %param.24, s32[]{:T(128)S(6)} %select_n.105, ...), kind=kLoop, calls=%fused_computation.49 | loop fusion | bytes 6291480 | tf_op jit(solution)/shard_map/dynamic_slice | solution.py:258
  28.7 5.0 %all-to-all-done = f32[32,1,384]{2,1,0:T(1,128)S(1)} async-done(((f32[32,1,384]{2,1,0:T(1,128)}), f32[32,1,384]{2,1,0:T(1,128)S(1)}, u32[]{:S(2)}, u32[]{:S(2)}) %all-to-all-start) | async-done | bytes 49184 | tf_op jit(solution)/shard_map/all_to_all | solution.py:279
  34.4 3.0 %collective-permute-start.4 = (bf16[256,1024]{1,0:T(8,128)(2,1)S(1)}, bf16[256,1024]{1,0:T(8,128)(2,1)S(1)}, u32[]{:S(2)}, u32[]{:S(2)}) collective-permute-start(bf16[256,1024]{1,0:T(8,128)(2,1)S(1)} %get-tuple-element.44), channel_id=1, source_target_pairs={{0,25},{1,24},{8,1},{9,0},{16,9},{17,8},{24,17},{25,16},{2,27},{3,... | collective-permute-start | bytes 1572872 | tf_op jit(solution)/shard_map/ppermute | solution.py:266
  37.6 1.0 fusion
  39.1 1.2 reduce.18
  40.3 1.5 reshape.124
  41.8 3.8 %all-to-all-start.1 = ((bf16[32,2,640]{2,1,0:T(2,128)(2,1)}), bf16[32,2,640]{2,1,0:T(2,128)(2,1)S(1)}, u32[]{:S(2)}, u32[]{:S(2)}) async-start(bf16[32,2,640]{2,1,0:T(2,128)(2,1)} %reshape.124), calls=%async_computation.1 | async-start | bytes 163840 | tf_op jit(solution)/shard_map/all_to_all | solution.py:303
  45.7 14.1 %all-to-all-done.1 = bf16[32,2,640]{2,1,0:T(2,128)(2,1)S(1)} async-done(((bf16[32,2,640]{2,1,0:T(2,128)(2,1)}), bf16[32,2,640]{2,1,0:T(2,128)(2,1)S(1)}, u32[]{:S(2)}, u32[]{:S(2)}) %all-to-all-start.1) | async-done | bytes 81952 | tf_op jit(solution)/shard_map/all_to_all | solution.py:303
  59.8 0.7 reshape.125
  61.0 1.1 collective-permute-start.7
  62.1 2.7 %collective-permute-start.8 = (bf16[256,1024]{1,0:T(8,128)(2,1)}, bf16[256,1024]{1,0:T(8,128)(2,1)}, u32[]{:S(2)}, u32[]{:S(2)}) collective-permute-start(bf16[256,1024]{1,0:T(8,128)(2,1)} %get-tuple-element.55), channel_id=1, source_target_pairs={{0,17},{1,16},{8,25},{9,24},{16,1},{17,0},{24,9},{25,8},{2,19},{3,... | collective-permute-start | bytes 1572872 | tf_op jit(solution)/shard_map/ppermute | solution.py:266
  64.8 0.8 multiply_cosine_fusion
  65.6 0.7 copy.35.lengths_ref
  66.9 1.7 convolution_convert_fusion.1.picked_ref
  68.6 10.8 %shard_map.136 = bf16[16,16,1024]{2,1,0:T(8,128)(2,1)} custom-call(bf16[8,512,1024]{2,1,0:T(8,128)(2,1)} %bitcast.41, bf16[8192,256]{1,0:T(8,128)(2,1)} %weight_ref.1, f32[8,1,1024]{2,1,0:T(1,128)} %bitcast.49, f32[2,512,128]{2,1,0:T(8,128)} %constant.204.clone.key_turns_ref, bf16[16,1280]{1,0:T(8,128)(2,1)} %convolution_convert_fusion.1.picked_ref, ...), custom_call_target="tpu_custom_call" | custom-call | tf_op jit(solution)/shard_map/pallas_call | solution.py:344
  79.5 3.1 %collective-permute-done.8.refs_7_ = bf16[256,1024]{1,0:T(8,128)(2,1)} collective-permute-done((bf16[256,1024]{1,0:T(8,128)(2,1)}, bf16[256,1024]{1,0:T(8,128)(2,1)}, u32[]{:S(2)}, u32[]{:S(2)}) %collective-permute-start.8) | collective-permute-done | bytes 524320 | tf_op jit(solution)/shard_map/ppermute | solution.py:266
  82.6 5.8 %all-to-all-start.2 = ((bf16[16,16,1024]{2,1,0:T(8,128)(2,1)}), bf16[16,16,1024]{2,1,0:T(8,128)(2,1)S(1)}, u32[]{:S(2)}, u32[]{:S(2)}) async-start(bf16[16,16,1024]{2,1,0:T(8,128)(2,1)} %shard_map.136), calls=%async_computation.2 | async-start | bytes 1048576 | tf_op jit(solution)/shard_map/all_to_all | solution.py:371
  89.0 13.1 %all-to-all-done.2.rows_ref = bf16[16,16,1024]{2,1,0:T(8,128)(2,1)S(1)} async-done(((bf16[16,16,1024]{2,1,0:T(8,128)(2,1)}), bf16[16,16,1024]{2,1,0:T(8,128)(2,1)S(1)}, u32[]{:S(2)}, u32[]{:S(2)}) %all-to-all-start.2) | async-done | bytes 524320 | tf_op jit(solution)/shard_map/all_to_all | solution.py:371
  102.1 1.0 shard_map.137
  103.0 7.7 %collective-permute-start.9 = (f32[16,8,512]{2,1,0:T(8,128)S(1)}, f32[16,8,512]{2,1,0:T(8,128)S(1)}, u32[]{:S(2)}, u32[]{:S(2)}) collective-permute-start(f32[16,8,512]{2,1,0:T(8,128)S(1)} %get-tuple-element.66), channel_id=1, source_target_pairs={{0,32},{32,0},{1,33},{33,1},{2,34},{34,2},{3,35},{35,3},{4,36},{36... | collective-permute-start | bytes 786440 | tf_op jit(solution)/shard_map/ppermute | solution.py:40
  110.9 0.8 collective-permute-start.5
  112.1 1.4 collective-permute-start.10
  113.5 2.6 %collective-permute-start.11 = (f32[32,512]{1,0:T(8,128)S(1)}, f32[32,512]{1,0:T(8,128)S(1)}, u32[]{:S(2)}, u32[]{:S(2)}) collective-permute-start(f32[32,512]{1,0:T(8,128)S(1)} %get-tuple-element.95), channel_id=1, source_target_pairs={{0,128},{64,192},{128,0},{192,64},{1,129},{65,193},{129,1},{193,65... | collective-permute-start | bytes 196616 | tf_op jit(solution)/shard_map/ppermute | solution.py:40
  116.1 1.1 collective-permute-start.12
  117.2 1.9 collective-permute-done.11
  119.7 18.6 %all_to_all.25 = bf16[32,32,512]{2,1,0:T(8,128)(2,1)S(1)} all-to-all(bf16[32,32,512]{2,1,0:T(8,128)(2,1)S(1)} %broadcast_in_dim.16), channel_id=1, replica_groups=mesh['y'=4,'c'=2,'x'=4,'h'=4,'l'=2] {'x','l','y'}, dimensions={0} | all-to-all | bytes 2097152 | tf_op jit(solution)/shard_map/all_to_all | solution.py:391
  138.3 3.0 %collective-permute-start.13 = (bf16[4,256,512]{2,1,0:T(8,128)(2,1)S(1)}, bf16[4,256,512]{2,1,0:T(8,128)(2,1)S(1)}, u32[]{:S(2)}, u32[]{:S(2)}) collective-permute-start(bf16[4,256,512]{2,1,0:T(8,128)(2,1)S(1)} %bitcast.42), channel_id=1, source_target_pairs={{0,32},{32,0},{1,33},{33,1},{2,34},{34,2},{3,35},{35,3},{4,36},{36... | collective-permute-start | bytes 3145736 | tf_op jit(solution)/shard_map/ppermute | solution.py:40
  141.4 0.7 broadcast_in_dim_reshape.2.order_ref
  142.7 0.9 collective-permute-done.13.refs_1_
  143.6 1.0 copy-done.4
  144.6 7.3 %shard_map.138 = (bf16[128,1152]{1,0:T(8,128)(2,1)}, bf16[128,1152]{1,0:T(8,128)(2,1)}, bf16[128,1152]{1,0:T(8,128)(2,1)}, bf16[128,1152]{1,0:T(8,128)(2,1)}) custom-call(s32[4]{0:T(128)} %copy-done.2, f32[4,1,512]{2,1,0:T(1,128)} %constant_dynamic-slice_fusion.7.gains_ref, s32[1,512]{1,0:T(1,128)} %broadcast_in_dim_reshape.2.order_ref, ...), custom_call_target="tpu_custom_call" | custom-call | tf_op jit(solution)/shard_map/pallas_call | solution.py:401
  151.9 1.1 collective-permute-start.14
  153.0 2.2 %collective-permute-start.15 = (bf16[128,1152]{1,0:T(8,128)(2,1)}, bf16[128,1152]{1,0:T(8,128)(2,1)S(1)}, u32[]{:S(2)}, u32[]{:S(2)}) collective-permute-start(bf16[128,1152]{1,0:T(8,128)(2,1)} %get-tuple-element.77), channel_id=1, source_target_pairs={{0,2},{2,4},{4,6},{6,0},{1,3},{3,5},{5,7},{7,1},{8,10},{10,12},{12... | collective-permute-start | bytes 884744 | tf_op jit(solution)/shard_map/ppermute | solution.py:40
  155.2 1.3 collective-permute-start.16
  157.1 0.7 reduce.17
  157.9 8.9 %collective-permute-done.14 = bf16[128,1152]{1,0:T(8,128)(2,1)S(1)} collective-permute-done((bf16[128,1152]{1,0:T(8,128)(2,1)}, bf16[128,1152]{1,0:T(8,128)(2,1)S(1)}, u32[]{:S(2)}, u32[]{:S(2)}) %collective-permute-start.14) | collective-permute-done | bytes 294944 | tf_op jit(solution)/shard_map/ppermute | solution.py:40
  166.8 9.6 %collective-permute-done.15 = bf16[128,1152]{1,0:T(8,128)(2,1)S(1)} collective-permute-done((bf16[128,1152]{1,0:T(8,128)(2,1)}, bf16[128,1152]{1,0:T(8,128)(2,1)S(1)}, u32[]{:S(2)}, u32[]{:S(2)}) %collective-permute-start.15) | collective-permute-done | bytes 294944 | tf_op jit(solution)/shard_map/ppermute | solution.py:40
  176.4 6.0 %collective-permute-done.16 = bf16[128,1152]{1,0:T(8,128)(2,1)S(1)} collective-permute-done((bf16[128,1152]{1,0:T(8,128)(2,1)}, bf16[128,1152]{1,0:T(8,128)(2,1)S(1)}, u32[]{:S(2)}, u32[]{:S(2)}) %collective-permute-start.16) | collective-permute-done | bytes 294944 | tf_op jit(solution)/shard_map/ppermute | solution.py:40
  182.4 1.1 convert_add_fusion
  184.4 13.6 %all_to_all.26 = f32[64,1,128]{2,1,0:T(1,128)S(1)} all-to-all(f32[64,1,128]{2,1,0:T(1,128)S(1)} %bitcast.47), channel_id=1, replica_groups=mesh['y'=4,'c'=2,'x'=4,'h'=4,'l'=2] {'y','c','x','l'}, dimensions={0} | all-to-all | bytes 65536 | tf_op jit(solution)/shard_map/all_to_all | solution.py:427
  (88 shorter events, 7.8 us)
Async XLA Ops:
  6.5 82.3 %copy-start = (bf16[1,512,256]{2,1,0:T(8,128)(2,1)S(1)}, bf16[1,512,256]{2,1,0:T(8,128)(2,1)}, u32[]{:S(2)}) copy-start(bf16[1,512,256]{2,1,0:T(8,128)(2,1)} %param.22) | copy-start | bytes 786436
  6.5 62.1 %all-gather.3.cloned.1.call-start = ((), (), s32[]{:S(2)}) async-start(), calls=%async_computation.5 | async-start | bytes 9437184 | tf_op jit(solution)/shard_map/all_gather | solution.py:249
  7.3 30.3 %copy-start.10 = (bf16[1,16,256]{2,1,0:T(8,128)(2,1)S(1)}, bf16[1,16,256]{2,1,0:T(8,128)(2,1)}, u32[]{:S(2)}) copy-start(bf16[1,16,256]{2,1,0:T(8,128)(2,1)} %param.20) | copy-start | bytes 24580
  7.3 38.4 %copy-start.12 = (s32[16]{0:T(128)S(1)}, s32[16]{0:T(128)}, u32[]{:S(2)}) copy-start(s32[16]{0:T(128)} %param.17) | copy-start | bytes 196
  8.6 25.1 %collective-permute-start = (bf16[256,1024]{1,0:T(8,128)(2,1)S(1)}, bf16[256,1024]{1,0:T(8,128)(2,1)S(1)}, u32[]{:S(2)}, u32[]{:S(2)}) collective-permute-start(bf16[256,1024]{1,0:T(8,128)(2,1)S(1)} %get-tuple-element.92), channel_id=1, source_target_pairs={{0,8},{1,9},{8,16},{9,17},{16,24},{17,25},{24,0},{25,1},{2,10},{3,... | collective-permute-start | bytes 1572872 | tf_op jit(solution)/shard_map/ppermute | solution.py:266
  10.7 23.0 %collective-permute-start.1 = (bf16[256,1024]{1,0:T(8,128)(2,1)S(1)}, bf16[256,1024]{1,0:T(8,128)(2,1)S(1)}, u32[]{:S(2)}, u32[]{:S(2)}) collective-permute-start(bf16[256,1024]{1,0:T(8,128)(2,1)S(1)} %get-tuple-element.91), channel_id=1, source_target_pairs={{0,24},{1,25},{8,0},{9,1},{16,8},{17,9},{24,16},{25,17},{2,26},{3,... | collective-permute-start | bytes 1572872 | tf_op jit(solution)/shard_map/ppermute | solution.py:266
  12.1 21.6 %collective-permute-start.2 = (bf16[1024,256]{1,0:T(8,128)(2,1)}, bf16[1024,256]{1,0:T(8,128)(2,1)S(1)}, u32[]{:S(2)}, u32[]{:S(2)}) collective-permute-start(bf16[1024,256]{1,0:T(8,128)(2,1)} %mine_ref.1), channel_id=1, source_target_pairs={{0,1},{1,0},{2,3},{3,2},{4,5},{5,4},{6,7},{7,6},{8,9},{9,8},{10,11... | collective-permute-start | bytes 1572872 | tf_op jit(solution)/shard_map/ppermute | solution.py:40
  15.9 17.7 %all-to-all-start = ((f32[32,1,384]{2,1,0:T(1,128)}), f32[32,1,384]{2,1,0:T(1,128)S(1)}, u32[]{:S(2)}, u32[]{:S(2)}) async-start(f32[32,1,384]{2,1,0:T(1,128)} %broadcast_in_dim.13), calls=%async_computation | async-start | bytes 98304 | tf_op jit(solution)/shard_map/all_to_all | solution.py:279
  33.7 45.7 %copy-start.5 = (bf16[256,1024]{1,0:T(8,128)(2,1)}, bf16[256,1024]{1,0:T(8,128)(2,1)S(1)}, u32[]{:S(2)}) copy-start(bf16[256,1024]{1,0:T(8,128)(2,1)S(1)} %collective-permute-done.refs_4_) | copy-start | bytes 1572868
  33.7 34.9 %copy-start.6 = (bf16[256,1024]{1,0:T(8,128)(2,1)}, bf16[256,1024]{1,0:T(8,128)(2,1)S(1)}, u32[]{:S(2)}) copy-start(bf16[256,1024]{1,0:T(8,128)(2,1)S(1)} %collective-permute-done.1.refs_8_) | copy-start | bytes 1572868
  33.7 26.8 %collective-permute-start.3 = (bf16[256,1024]{1,0:T(8,128)(2,1)}, bf16[256,1024]{1,0:T(8,128)(2,1)S(1)}, u32[]{:S(2)}, u32[]{:S(2)}) collective-permute-start(bf16[256,1024]{1,0:T(8,128)(2,1)} %get-tuple-element.43), channel_id=1, source_target_pairs={{0,9},{1,8},{8,17},{9,16},{16,25},{17,24},{24,1},{25,0},{2,11},{3,... | collective-permute-start | bytes 1572872 | tf_op jit(solution)/shard_map/ppermute | solution.py:266
  34.4 26.2 %collective-permute-start.4 = (bf16[256,1024]{1,0:T(8,128)(2,1)S(1)}, bf16[256,1024]{1,0:T(8,128)(2,1)S(1)}, u32[]{:S(2)}, u32[]{:S(2)}) collective-permute-start(bf16[256,1024]{1,0:T(8,128)(2,1)S(1)} %get-tuple-element.44), channel_id=1, source_target_pairs={{0,25},{1,24},{8,1},{9,0},{16,9},{17,8},{24,17},{25,16},{2,27},{3,... | collective-permute-start | bytes 1572872 | tf_op jit(solution)/shard_map/ppermute | solution.py:266
  41.8 17.9 %all-to-all-start.1 = ((bf16[32,2,640]{2,1,0:T(2,128)(2,1)}), bf16[32,2,640]{2,1,0:T(2,128)(2,1)S(1)}, u32[]{:S(2)}, u32[]{:S(2)}) async-start(bf16[32,2,640]{2,1,0:T(2,128)(2,1)} %reshape.124), calls=%async_computation.1 | async-start | bytes 163840 | tf_op jit(solution)/shard_map/all_to_all | solution.py:303
  60.5 18.9 %copy-start.7 = (bf16[256,1024]{1,0:T(8,128)(2,1)}, bf16[256,1024]{1,0:T(8,128)(2,1)S(1)}, u32[]{:S(2)}) copy-start(bf16[256,1024]{1,0:T(8,128)(2,1)S(1)} %collective-permute-done.3.refs_5_) | copy-start | bytes 1572868
  60.5 18.9 %copy-start.8 = (bf16[256,1024]{1,0:T(8,128)(2,1)}, bf16[256,1024]{1,0:T(8,128)(2,1)S(1)}, u32[]{:S(2)}) copy-start(bf16[256,1024]{1,0:T(8,128)(2,1)S(1)} %collective-permute-done.4.refs_9_) | copy-start | bytes 1572868
  60.5 18.9 %collective-permute-start.6 = (bf16[256,1024]{1,0:T(8,128)(2,1)}, bf16[256,1024]{1,0:T(8,128)(2,1)S(1)}, u32[]{:S(2)}, u32[]{:S(2)}) collective-permute-start(bf16[256,1024]{1,0:T(8,128)(2,1)} %get-tuple-element.53), channel_id=1, source_target_pairs={{0,1},{1,0},{8,9},{9,8},{16,17},{17,16},{24,25},{25,24},{2,3},{3,2... | collective-permute-start | bytes 1572872 | tf_op jit(solution)/shard_map/ppermute | solution.py:266
  61.0 18.4 %collective-permute-start.7 = (bf16[256,1024]{1,0:T(8,128)(2,1)}, bf16[256,1024]{1,0:T(8,128)(2,1)}, u32[]{:S(2)}, u32[]{:S(2)}) collective-permute-start(bf16[256,1024]{1,0:T(8,128)(2,1)} %get-tuple-element.54), channel_id=1, source_target_pairs={{0,16},{1,17},{8,24},{9,25},{16,0},{17,1},{24,8},{25,9},{2,18},{3,... | collective-permute-start | bytes 1572872 | tf_op jit(solution)/shard_map/ppermute | solution.py:266
  62.1 20.5 %collective-permute-start.8 = (bf16[256,1024]{1,0:T(8,128)(2,1)}, bf16[256,1024]{1,0:T(8,128)(2,1)}, u32[]{:S(2)}, u32[]{:S(2)}) collective-permute-start(bf16[256,1024]{1,0:T(8,128)(2,1)} %get-tuple-element.55), channel_id=1, source_target_pairs={{0,17},{1,16},{8,25},{9,24},{16,1},{17,0},{24,9},{25,8},{2,19},{3,... | collective-permute-start | bytes 1572872 | tf_op jit(solution)/shard_map/ppermute | solution.py:266
  68.6 33.4 %copy-start.1 = (bf16[1024,256]{1,0:T(8,128)(2,1)S(1)}, bf16[1024,256]{1,0:T(8,128)(2,1)}, u32[]{:S(2)}) copy-start(bf16[1024,256]{1,0:T(8,128)(2,1)} %mine_ref.1) | copy-start | bytes 1572868
  79.5 9.5 %copy-start.9 = (bf16[256,1024]{1,0:T(8,128)(2,1)}, bf16[256,1024]{1,0:T(8,128)(2,1)S(1)}, u32[]{:S(2)}) copy-start(bf16[256,1024]{1,0:T(8,128)(2,1)S(1)} %collective-permute-done.6.refs_3_) | copy-start | bytes 1572868
  82.6 19.4 %all-to-all-start.2 = ((bf16[16,16,1024]{2,1,0:T(8,128)(2,1)}), bf16[16,16,1024]{2,1,0:T(8,128)(2,1)S(1)}, u32[]{:S(2)}, u32[]{:S(2)}) async-start(bf16[16,16,1024]{2,1,0:T(8,128)(2,1)} %shard_map.136), calls=%async_computation.2 | async-start | bytes 1048576 | tf_op jit(solution)/shard_map/all_to_all | solution.py:371
  88.5 55.1 %copy-start.2 = (s32[4]{0:T(128)}, s32[4]{0:T(128)S(1)}, u32[]{:S(2)}) copy-start(s32[4]{0:T(128)S(1)} %pad_add_fusion.place_ref) | copy-start | bytes 52
  103.0 9.0 %collective-permute-start.9 = (f32[16,8,512]{2,1,0:T(8,128)S(1)}, f32[16,8,512]{2,1,0:T(8,128)S(1)}, u32[]{:S(2)}, u32[]{:S(2)}) collective-permute-start(f32[16,8,512]{2,1,0:T(8,128)S(1)} %get-tuple-element.66), channel_id=1, source_target_pairs={{0,32},{32,0},{1,33},{33,1},{2,34},{34,2},{3,35},{35,3},{4,36},{36... | collective-permute-start | bytes 786440 | tf_op jit(solution)/shard_map/ppermute | solution.py:40
  110.9 6.3 %collective-permute-start.5 = (bf16[32,256]{1,0:T(8,128)(2,1)S(1)}, bf16[32,256]{1,0:T(8,128)(2,1)S(1)}, u32[]{:S(2)}, u32[]{:S(2)}) collective-permute-start(bf16[32,256]{1,0:T(8,128)(2,1)S(1)} %convolution_convert_fusion.2), channel_id=1, source_target_pairs={{0,1},{1,0},{2,3},{3,2},{4,5},{5,4},{6,7},{7,6},{8,9},{9,8},{10,11... | collective-permute-start | bytes 49160 | tf_op jit(solution)/shard_map/ppermute | solution.py:40
  112.1 5.1 %collective-permute-start.10 = (f32[32,512]{1,0:T(8,128)S(1)}, f32[32,512]{1,0:T(8,128)S(1)}, u32[]{:S(2)}, u32[]{:S(2)}) collective-permute-start(f32[32,512]{1,0:T(8,128)S(1)} %get-tuple-element.93), channel_id=1, source_target_pairs={{0,64},{64,128},{128,192},{192,0},{1,65},{65,129},{129,193},{193,1... | collective-permute-start | bytes 196616 | tf_op jit(solution)/shard_map/ppermute | solution.py:40
  113.5 5.7 %collective-permute-start.11 = (f32[32,512]{1,0:T(8,128)S(1)}, f32[32,512]{1,0:T(8,128)S(1)}, u32[]{:S(2)}, u32[]{:S(2)}) collective-permute-start(f32[32,512]{1,0:T(8,128)S(1)} %get-tuple-element.95), channel_id=1, source_target_pairs={{0,128},{64,192},{128,0},{192,64},{1,129},{65,193},{129,1},{193,65... | collective-permute-start | bytes 196616 | tf_op jit(solution)/shard_map/ppermute | solution.py:40
  116.1 3.4 %collective-permute-start.12 = (f32[32,512]{1,0:T(8,128)S(1)}, f32[32,512]{1,0:T(8,128)S(1)}, u32[]{:S(2)}, u32[]{:S(2)}) collective-permute-start(f32[32,512]{1,0:T(8,128)S(1)} %get-tuple-element.94), channel_id=1, source_target_pairs={{0,192},{64,0},{128,64},{192,128},{1,193},{65,1},{129,65},{193,129... | collective-permute-start | bytes 196616 | tf_op jit(solution)/shard_map/ppermute | solution.py:40
  119.7 37.4 %copy-start.11 = (s32[1,512]{1,0:T(1,128)S(1)}, s32[1,512]{1,0:T(1,128)}, u32[]{:S(2)}) copy-start(s32[1,512]{1,0:T(1,128)} %param.25) | copy-start | bytes 6148
  138.3 5.3 %copy-start.3 = (bf16[32,32,512]{2,1,0:T(8,128)(2,1)}, bf16[32,32,512]{2,1,0:T(8,128)(2,1)S(1)}, u32[]{:S(2)}) copy-start(bf16[32,32,512]{2,1,0:T(8,128)(2,1)S(1)} %all_to_all.25) | copy-start | bytes 3145732
  138.3 5.3 %collective-permute-start.13 = (bf16[4,256,512]{2,1,0:T(8,128)(2,1)S(1)}, bf16[4,256,512]{2,1,0:T(8,128)(2,1)S(1)}, u32[]{:S(2)}, u32[]{:S(2)}) collective-permute-start(bf16[4,256,512]{2,1,0:T(8,128)(2,1)S(1)} %bitcast.42), channel_id=1, source_target_pairs={{0,32},{32,0},{1,33},{33,1},{2,34},{34,2},{3,35},{35,3},{4,36},{36... | collective-permute-start | bytes 3145736 | tf_op jit(solution)/shard_map/ppermute | solution.py:40
  143.6 1.0 copy-start.4
  151.9 14.9 %collective-permute-start.14 = (bf16[128,1152]{1,0:T(8,128)(2,1)}, bf16[128,1152]{1,0:T(8,128)(2,1)S(1)}, u32[]{:S(2)}, u32[]{:S(2)}) collective-permute-start(bf16[128,1152]{1,0:T(8,128)(2,1)} %get-tuple-element.76), channel_id=1, source_target_pairs={{0,4},{2,6},{4,0},{6,2},{1,5},{3,7},{5,1},{7,3},{8,12},{10,14},{12... | collective-permute-start | bytes 884744 | tf_op jit(solution)/shard_map/ppermute | solution.py:40
  153.0 23.4 %collective-permute-start.15 = (bf16[128,1152]{1,0:T(8,128)(2,1)}, bf16[128,1152]{1,0:T(8,128)(2,1)S(1)}, u32[]{:S(2)}, u32[]{:S(2)}) collective-permute-start(bf16[128,1152]{1,0:T(8,128)(2,1)} %get-tuple-element.77), channel_id=1, source_target_pairs={{0,2},{2,4},{4,6},{6,0},{1,3},{3,5},{5,7},{7,1},{8,10},{10,12},{12... | collective-permute-start | bytes 884744 | tf_op jit(solution)/shard_map/ppermute | solution.py:40
  155.2 27.1 %collective-permute-start.16 = (bf16[128,1152]{1,0:T(8,128)(2,1)}, bf16[128,1152]{1,0:T(8,128)(2,1)S(1)}, u32[]{:S(2)}, u32[]{:S(2)}) collective-permute-start(bf16[128,1152]{1,0:T(8,128)(2,1)} %get-tuple-element.78), channel_id=1, source_target_pairs={{0,6},{2,0},{4,2},{6,4},{1,7},{3,1},{5,3},{7,5},{8,14},{10,8},{12,... | collective-permute-start | bytes 884744 | tf_op jit(solution)/shard_map/ppermute | solution.py:40
Sparse Core Ops, SparseCore 0:
  9.2 56.5 all-gather.2

commit v2 on v1

--- a/solution.py
+++ b/solution.py
@@ -301,7 +301,7 @@
     wanted = jnp.any(owners == own_rows[None, :, None], axis=2).astype(bf16)
     outgoing = dot(wanted, decode_rows).astype(bf16)
     incoming = lax.all_to_all(outgoing[:, None, :], wide_axes, 0, 0, tiled=True)
-    told, incoming = phase([(1, 1), (3, 1)], told, incoming)
+    told, incoming = phase([(1, 1), (3, 1), (2, 0)], told, incoming)
     owners = told[:, :, :requests].astype(jnp.int32)
     gains = told[:, 0, requests : requests + columns]
     gains = gains.reshape(x_count, high_count, low_count * columns)
@@ -367,7 +367,7 @@
         prompt_lengths[:, None],
     )
 
-    (attended,) = phase([(2, 0), (2, 1), (0, 1)], attended)
+    (attended,) = phase([(2, 1), (0, 1)], attended)
     attended = lax.all_to_all(attended, ("x", "h"), 0, 0, tiled=True)
     place = jnp.stack([core, low, x, high]).astype(jnp.int32)
     smem = pl.BlockSpec(memory_space=pltpu.SMEM)

time: 206 us -> 206 us (level)
  waiting for transfers between devices: 63.6 us -> 68.2 us
  starting transfers between devices: 52.9 us -> 48.9 us
    ppermute x7, waiting for transfers between devices: 3.16 us -> 6.29 us  [moved(): return lax.ppermute(block, ('x', 'l'), pairs)]
where the time goes in v2:
time: 206 us; the launch traced here: 205 us
  waiting for transfers between devices  68.2 us (33%)
  starting transfers between devices  48.9 us (24%)
  blocking collectives  31.4 us (15%)
  Pallas kernels  19 us (9%)
  between operations  13.9 us (7%)
  local copies, waits for them, and re-layouts  13.5 us (7%)
  other arithmetic  7.57 us (4%)
  matrix products  3.07 us (1%)
    ppermute x10, waiting for transfers between devices, shift(): lax.ppermute(value, axis, [(i, (i + step) % count) for i in range(count)])  28.2 us
    ppermute x10, starting transfers between devices, shift(): lax.ppermute(value, axis, [(i, (i + step) % count) for i in range(count)])  22.3 us
    all_to_all x1, blocking collectives, local(): lax.all_to_all(jnp.broadcast_to(gained[None], (count,) + gained.shape), (...  18.4 us
    all_to_all x1, waiting for transfers between devices, local(): incoming = lax.all_to_all(outgoing[:, None, :], wide_axes, 0, 0, tiled=True)  15.2 us
    all_to_all x1, blocking collectives, local(): stats = lax.all_to_all(stats, ('y', 'c', 'x', 'l'), 0, 0, tiled=True)[:, 0]  13 us
    all_to_all x1, waiting for transfers between devices, local(): attended = lax.all_to_all(attended, ('x', 'h'), 0, 0, tiled=True)  12.9 us
    pallas_call x1, Pallas kernels, local(): pl.pallas_call(functools.partial(attend_kernel, width, cache_len), grid=(...  10.8 us
    ppermute x7, starting transfers between devices, moved(): return lax.ppermute(block, ('x', 'l'), pairs)  9.56 us
  transfers between devices with their start and end apart: 21, of which 10 were waited for; matrix products, arithmetic and copies ran while one was open for 10% of the time, Pallas kernels for 5%

profile of v2, /device:TPU:1, one launch (start us, length us, event | category | flops | bytes accessed | tf_op | source)
XLA Modules:
  0.0 205.5 jit_solution(18136085261216884338)
XLA Ops:
  6.5 0.7 all-gather.3.cloned.1.call-update
  7.3 1.3 constant_dynamic-slice_fusion.14
  8.6 2.1 %collective-permute-start = (bf16[256,1024]{1,0:T(8,128)(2,1)S(1)}, bf16[256,1024]{1,0:T(8,128)(2,1)S(1)}, u32[]{:S(2)}, u32[]{:S(2)}) collective-permute-start(bf16[256,1024]{1,0:T(8,128)(2,1)S(1)} %get-tuple-element.92), channel_id=1, source_target_pairs={{0,8},{1,9},{8,16},{9,17},{16,24},{17,25},{24,0},{25,1},{2,10},{3,... | collective-permute-start | bytes 1572872 | tf_op jit(solution)/shard_map/ppermute | solution.py:266
  10.7 1.4 collective-permute-start.1
  12.1 1.7 collective-permute-start.2
  13.8 0.7 and_select_fusion
  14.5 0.8 select_maximum_fusion
  15.9 8.9 %all-to-all-start = ((f32[32,1,384]{2,1,0:T(1,128)}), f32[32,1,384]{2,1,0:T(1,128)S(1)}, u32[]{:S(2)}, u32[]{:S(2)}) async-start(f32[32,1,384]{2,1,0:T(1,128)} %broadcast_in_dim.13), calls=%async_computation | async-start | bytes 98304 | tf_op jit(solution)/shard_map/all_to_all | solution.py:279
  24.9 3.9 %constant_dynamic-slice_fusion.8 = (bf16[256,1024]{1,0:T(8,128)(2,1)}, bf16[256,1024]{1,0:T(8,128)(2,1)}, bf16[256,1024]{1,0:T(8,128)(2,1)}, bf16[256,1024]{1,0:...) fusion(bf16[256,8192]{1,0:T(8,128)(2,1)} %param.24, s32[]{:T(128)S(6)} %select_n.105, ...), kind=kLoop, calls=%fused_computation.49 | loop fusion | bytes 6291480 | tf_op jit(solution)/shard_map/dynamic_slice | solution.py:258
  28.8 4.8 %all-to-all-done = f32[32,1,384]{2,1,0:T(1,128)S(1)} async-done(((f32[32,1,384]{2,1,0:T(1,128)}), f32[32,1,384]{2,1,0:T(1,128)S(1)}, u32[]{:S(2)}, u32[]{:S(2)}) %all-to-all-start) | async-done | bytes 49184 | tf_op jit(solution)/shard_map/all_to_all | solution.py:279
  34.4 1.7 collective-permute-start.4
  36.1 1.7 collective-permute-start.5
  38.0 1.0 fusion
  39.5 1.3 reduce.18
  40.8 1.6 reshape.124
  42.4 4.3 %all-to-all-start.1 = ((bf16[32,2,640]{2,1,0:T(2,128)(2,1)}), bf16[32,2,640]{2,1,0:T(2,128)(2,1)S(1)}, u32[]{:S(2)}, u32[]{:S(2)}) async-start(bf16[32,2,640]{2,1,0:T(2,128)(2,1)} %reshape.124), calls=%async_computation.1 | async-start | bytes 163840 | tf_op jit(solution)/shard_map/all_to_all | solution.py:303
  46.6 15.2 %all-to-all-done.1 = bf16[32,2,640]{2,1,0:T(2,128)(2,1)S(1)} async-done(((bf16[32,2,640]{2,1,0:T(2,128)(2,1)}), bf16[32,2,640]{2,1,0:T(2,128)(2,1)S(1)}, u32[]{:S(2)}, u32[]{:S(2)}) %all-to-all-start.1) | async-done | bytes 81952 | tf_op jit(solution)/shard_map/all_to_all | solution.py:303
  61.9 0.7 reshape.125
  63.3 1.4 collective-permute-start.8
  64.6 0.8 multiply_cosine_fusion
  65.4 0.7 copy.35.lengths_ref
  66.8 1.7 convolution_convert_fusion.1.picked_ref
  68.5 10.8 %shard_map.136 = bf16[16,16,1024]{2,1,0:T(8,128)(2,1)} custom-call(bf16[8,512,1024]{2,1,0:T(8,128)(2,1)} %bitcast.41, bf16[8192,256]{1,0:T(8,128)(2,1)} %weight_ref.1, f32[8,1,1024]{2,1,0:T(1,128)} %bitcast.49, f32[2,512,128]{2,1,0:T(8,128)} %constant.204.clone.key_turns_ref, bf16[16,1280]{1,0:T(8,128)(2,1)} %convolution_convert_fusion.1.picked_ref, ...), custom_call_target="tpu_custom_call" | custom-call | tf_op jit(solution)/shard_map/pallas_call | solution.py:344
  79.3 6.3 %collective-permute-done.8.refs_7_ = bf16[256,1024]{1,0:T(8,128)(2,1)} collective-permute-done((bf16[256,1024]{1,0:T(8,128)(2,1)}, bf16[256,1024]{1,0:T(8,128)(2,1)}, u32[]{:S(2)}, u32[]{:S(2)}) %collective-permute-start.8) | collective-permute-done | bytes 524320 | tf_op jit(solution)/shard_map/ppermute | solution.py:266
  85.6 3.9 %all-to-all-start.2 = ((bf16[16,16,1024]{2,1,0:T(8,128)(2,1)}), bf16[16,16,1024]{2,1,0:T(8,128)(2,1)S(1)}, u32[]{:S(2)}, u32[]{:S(2)}) async-start(bf16[16,16,1024]{2,1,0:T(8,128)(2,1)} %shard_map.136), calls=%async_computation.2 | async-start | bytes 1048576 | tf_op jit(solution)/shard_map/all_to_all | solution.py:371
  90.0 12.9 %all-to-all-done.2.rows_ref = bf16[16,16,1024]{2,1,0:T(8,128)(2,1)S(1)} async-done(((bf16[16,16,1024]{2,1,0:T(8,128)(2,1)}), bf16[16,16,1024]{2,1,0:T(8,128)(2,1)S(1)}, u32[]{:S(2)}, u32[]{:S(2)}) %all-to-all-start.2) | async-done | bytes 524320 | tf_op jit(solution)/shard_map/all_to_all | solution.py:371
  102.9 1.0 shard_map.137
  103.9 6.7 %collective-permute-start.9 = (f32[16,8,512]{2,1,0:T(8,128)S(1)}, f32[16,8,512]{2,1,0:T(8,128)S(1)}, u32[]{:S(2)}, u32[]{:S(2)}) collective-permute-start(f32[16,8,512]{2,1,0:T(8,128)S(1)} %get-tuple-element.66), channel_id=1, source_target_pairs={{0,32},{32,0},{1,33},{33,1},{2,34},{34,2},{3,35},{35,3},{4,36},{36... | collective-permute-start | bytes 786440 | tf_op jit(solution)/shard_map/ppermute | solution.py:40
  110.7 1.0 collective-permute-start.6
  112.1 1.4 collective-permute-start.10
  113.5 2.6 %collective-permute-start.11 = (f32[32,512]{1,0:T(8,128)S(1)}, f32[32,512]{1,0:T(8,128)S(1)}, u32[]{:S(2)}, u32[]{:S(2)}) collective-permute-start(f32[32,512]{1,0:T(8,128)S(1)} %get-tuple-element.95), channel_id=1, source_target_pairs={{0,128},{64,192},{128,0},{192,64},{1,129},{65,193},{129,1},{193,65... | collective-permute-start | bytes 196616 | tf_op jit(solution)/shard_map/ppermute | solution.py:40
  116.1 1.1 collective-permute-start.12
  117.2 1.9 collective-permute-done.11
  119.7 18.4 %all_to_all.25 = bf16[32,32,512]{2,1,0:T(8,128)(2,1)S(1)} all-to-all(bf16[32,32,512]{2,1,0:T(8,128)(2,1)S(1)} %broadcast_in_dim.16), channel_id=1, replica_groups=mesh['y'=4,'c'=2,'x'=4,'h'=4,'l'=2] {'x','l','y'}, dimensions={0} | all-to-all | bytes 2097152 | tf_op jit(solution)/shard_map/all_to_all | solution.py:391
  138.1 3.0 %collective-permute-start.13 = (bf16[4,256,512]{2,1,0:T(8,128)(2,1)S(1)}, bf16[4,256,512]{2,1,0:T(8,128)(2,1)S(1)}, u32[]{:S(2)}, u32[]{:S(2)}) collective-permute-start(bf16[4,256,512]{2,1,0:T(8,128)(2,1)S(1)} %bitcast.42), channel_id=1, source_target_pairs={{0,32},{32,0},{1,33},{33,1},{2,34},{34,2},{3,35},{35,3},{4,36},{36... | collective-permute-start | bytes 3145736 | tf_op jit(solution)/shard_map/ppermute | solution.py:40
  141.3 0.7 broadcast_in_dim_reshape.2.order_ref
  142.6 0.9 collective-permute-done.13.refs_1_
  143.5 1.0 copy-done.4
  144.5 7.3 %shard_map.138 = (bf16[128,1152]{1,0:T(8,128)(2,1)}, bf16[128,1152]{1,0:T(8,128)(2,1)}, bf16[128,1152]{1,0:T(8,128)(2,1)}, bf16[128,1152]{1,0:T(8,128)(2,1)}) custom-call(s32[4]{0:T(128)} %copy-done.2, f32[4,1,512]{2,1,0:T(1,128)} %constant_dynamic-slice_fusion.7.gains_ref, s32[1,512]{1,0:T(1,128)} %broadcast_in_dim_reshape.2.order_ref, ...), custom_call_target="tpu_custom_call" | custom-call | tf_op jit(solution)/shard_map/pallas_call | solution.py:401
  151.8 1.2 collective-permute-start.14
  153.0 2.7 %collective-permute-start.15 = (bf16[128,1152]{1,0:T(8,128)(2,1)}, bf16[128,1152]{1,0:T(8,128)(2,1)S(1)}, u32[]{:S(2)}, u32[]{:S(2)}) collective-permute-start(bf16[128,1152]{1,0:T(8,128)(2,1)} %get-tuple-element.77), channel_id=1, source_target_pairs={{0,2},{2,4},{4,6},{6,0},{1,3},{3,5},{5,7},{7,1},{8,10},{10,12},{12... | collective-permute-start | bytes 884744 | tf_op jit(solution)/shard_map/ppermute | solution.py:40
  155.7 0.8 collective-permute-start.16
  157.1 0.7 reduce.17
  157.9 7.9 %collective-permute-done.14 = bf16[128,1152]{1,0:T(8,128)(2,1)S(1)} collective-permute-done((bf16[128,1152]{1,0:T(8,128)(2,1)}, bf16[128,1152]{1,0:T(8,128)(2,1)S(1)}, u32[]{:S(2)}, u32[]{:S(2)}) %collective-permute-start.14) | collective-permute-done | bytes 294944 | tf_op jit(solution)/shard_map/ppermute | solution.py:40
  165.9 9.8 %collective-permute-done.15 = bf16[128,1152]{1,0:T(8,128)(2,1)S(1)} collective-permute-done((bf16[128,1152]{1,0:T(8,128)(2,1)}, bf16[128,1152]{1,0:T(8,128)(2,1)S(1)}, u32[]{:S(2)}, u32[]{:S(2)}) %collective-permute-start.15) | collective-permute-done | bytes 294944 | tf_op jit(solution)/shard_map/ppermute | solution.py:40
  175.7 7.3 %collective-permute-done.16 = bf16[128,1152]{1,0:T(8,128)(2,1)S(1)} collective-permute-done((bf16[128,1152]{1,0:T(8,128)(2,1)}, bf16[128,1152]{1,0:T(8,128)(2,1)S(1)}, u32[]{:S(2)}, u32[]{:S(2)}) %collective-permute-start.16) | collective-permute-done | bytes 294944 | tf_op jit(solution)/shard_map/ppermute | solution.py:40
  182.9 1.1 convert_add_fusion
  185.0 13.0 %all_to_all.26 = f32[64,1,128]{2,1,0:T(1,128)S(1)} all-to-all(f32[64,1,128]{2,1,0:T(1,128)S(1)} %bitcast.47), channel_id=1, replica_groups=mesh['y'=4,'c'=2,'x'=4,'h'=4,'l'=2] {'y','c','x','l'}, dimensions={0} | all-to-all | bytes 65536 | tf_op jit(solution)/shard_map/all_to_all | solution.py:427
  (88 shorter events, 7.9 us)
Async XLA Ops:
  6.5 83.3 %copy-start = (bf16[1,512,256]{2,1,0:T(8,128)(2,1)S(1)}, bf16[1,512,256]{2,1,0:T(8,128)(2,1)}, u32[]{:S(2)}) copy-start(bf16[1,512,256]{2,1,0:T(8,128)(2,1)} %param.22) | copy-start | bytes 786436
  6.5 61.9 %all-gather.3.cloned.1.call-start = ((), (), s32[]{:S(2)}) async-start(), calls=%async_computation.5 | async-start | bytes 9437184 | tf_op jit(solution)/shard_map/all_gather | solution.py:249
  7.3 30.8 %copy-start.10 = (bf16[1,16,256]{2,1,0:T(8,128)(2,1)S(1)}, bf16[1,16,256]{2,1,0:T(8,128)(2,1)}, u32[]{:S(2)}) copy-start(bf16[1,16,256]{2,1,0:T(8,128)(2,1)} %param.20) | copy-start | bytes 24580
  7.3 39.3 %copy-start.12 = (s32[16]{0:T(128)S(1)}, s32[16]{0:T(128)}, u32[]{:S(2)}) copy-start(s32[16]{0:T(128)} %param.17) | copy-start | bytes 196
  8.6 25.1 %collective-permute-start = (bf16[256,1024]{1,0:T(8,128)(2,1)S(1)}, bf16[256,1024]{1,0:T(8,128)(2,1)S(1)}, u32[]{:S(2)}, u32[]{:S(2)}) collective-permute-start(bf16[256,1024]{1,0:T(8,128)(2,1)S(1)} %get-tuple-element.92), channel_id=1, source_target_pairs={{0,8},{1,9},{8,16},{9,17},{16,24},{17,25},{24,0},{25,1},{2,10},{3,... | collective-permute-start | bytes 1572872 | tf_op jit(solution)/shard_map/ppermute | solution.py:266
  10.7 23.0 %collective-permute-start.1 = (bf16[256,1024]{1,0:T(8,128)(2,1)S(1)}, bf16[256,1024]{1,0:T(8,128)(2,1)S(1)}, u32[]{:S(2)}, u32[]{:S(2)}) collective-permute-start(bf16[256,1024]{1,0:T(8,128)(2,1)S(1)} %get-tuple-element.91), channel_id=1, source_target_pairs={{0,24},{1,25},{8,0},{9,1},{16,8},{17,9},{24,16},{25,17},{2,26},{3,... | collective-permute-start | bytes 1572872 | tf_op jit(solution)/shard_map/ppermute | solution.py:266
  12.1 21.6 %collective-permute-start.2 = (bf16[1024,256]{1,0:T(8,128)(2,1)}, bf16[1024,256]{1,0:T(8,128)(2,1)S(1)}, u32[]{:S(2)}, u32[]{:S(2)}) collective-permute-start(bf16[1024,256]{1,0:T(8,128)(2,1)} %mine_ref.1), channel_id=1, source_target_pairs={{0,1},{1,0},{2,3},{3,2},{4,5},{5,4},{6,7},{7,6},{8,9},{9,8},{10,11... | collective-permute-start | bytes 1572872 | tf_op jit(solution)/shard_map/ppermute | solution.py:40
  15.9 17.7 %all-to-all-start = ((f32[32,1,384]{2,1,0:T(1,128)}), f32[32,1,384]{2,1,0:T(1,128)S(1)}, u32[]{:S(2)}, u32[]{:S(2)}) async-start(f32[32,1,384]{2,1,0:T(1,128)} %broadcast_in_dim.13), calls=%async_computation | async-start | bytes 98304 | tf_op jit(solution)/shard_map/all_to_all | solution.py:279
  33.7 45.6 %copy-start.5 = (bf16[256,1024]{1,0:T(8,128)(2,1)}, bf16[256,1024]{1,0:T(8,128)(2,1)S(1)}, u32[]{:S(2)}) copy-start(bf16[256,1024]{1,0:T(8,128)(2,1)S(1)} %collective-permute-done.refs_4_) | copy-start | bytes 1572868
  33.7 34.8 %copy-start.6 = (bf16[256,1024]{1,0:T(8,128)(2,1)}, bf16[256,1024]{1,0:T(8,128)(2,1)S(1)}, u32[]{:S(2)}) copy-start(bf16[256,1024]{1,0:T(8,128)(2,1)S(1)} %collective-permute-done.1.refs_8_) | copy-start | bytes 1572868
  33.7 28.9 %collective-permute-start.3 = (bf16[256,1024]{1,0:T(8,128)(2,1)}, bf16[256,1024]{1,0:T(8,128)(2,1)S(1)}, u32[]{:S(2)}, u32[]{:S(2)}) collective-permute-start(bf16[256,1024]{1,0:T(8,128)(2,1)} %get-tuple-element.43), channel_id=1, source_target_pairs={{0,9},{1,8},{8,17},{9,16},{16,25},{17,24},{24,1},{25,0},{2,11},{3,... | collective-permute-start | bytes 1572872 | tf_op jit(solution)/shard_map/ppermute | solution.py:266
  34.4 28.3 %collective-permute-start.4 = (bf16[256,1024]{1,0:T(8,128)(2,1)}, bf16[256,1024]{1,0:T(8,128)(2,1)S(1)}, u32[]{:S(2)}, u32[]{:S(2)}) collective-permute-start(bf16[256,1024]{1,0:T(8,128)(2,1)} %get-tuple-element.44), channel_id=1, source_target_pairs={{0,16},{1,17},{8,24},{9,25},{16,0},{17,1},{24,8},{25,9},{2,18},{3,... | collective-permute-start | bytes 1572872 | tf_op jit(solution)/shard_map/ppermute | solution.py:266
  36.1 26.5 %collective-permute-start.5 = (bf16[256,1024]{1,0:T(8,128)(2,1)}, bf16[256,1024]{1,0:T(8,128)(2,1)S(1)}, u32[]{:S(2)}, u32[]{:S(2)}) collective-permute-start(bf16[256,1024]{1,0:T(8,128)(2,1)} %get-tuple-element.45), channel_id=1, source_target_pairs={{0,25},{1,24},{8,1},{9,0},{16,9},{17,8},{24,17},{25,16},{2,27},{3,... | collective-permute-start | bytes 1572872 | tf_op jit(solution)/shard_map/ppermute | solution.py:266
  42.4 19.5 %all-to-all-start.1 = ((bf16[32,2,640]{2,1,0:T(2,128)(2,1)}), bf16[32,2,640]{2,1,0:T(2,128)(2,1)S(1)}, u32[]{:S(2)}, u32[]{:S(2)}) async-start(bf16[32,2,640]{2,1,0:T(2,128)(2,1)} %reshape.124), calls=%async_computation.1 | async-start | bytes 163840 | tf_op jit(solution)/shard_map/all_to_all | solution.py:303
  62.6 16.6 %copy-start.7 = (bf16[256,1024]{1,0:T(8,128)(2,1)}, bf16[256,1024]{1,0:T(8,128)(2,1)S(1)}, u32[]{:S(2)}) copy-start(bf16[256,1024]{1,0:T(8,128)(2,1)S(1)} %collective-permute-done.3.refs_5_) | copy-start | bytes 1572868
  62.6 16.6 %copy-start.8 = (bf16[256,1024]{1,0:T(8,128)(2,1)}, bf16[256,1024]{1,0:T(8,128)(2,1)S(1)}, u32[]{:S(2)}) copy-start(bf16[256,1024]{1,0:T(8,128)(2,1)S(1)} %collective-permute-done.4.refs_6_) | copy-start | bytes 1572868
  62.6 16.6 %copy-start.9 = (bf16[256,1024]{1,0:T(8,128)(2,1)}, bf16[256,1024]{1,0:T(8,128)(2,1)S(1)}, u32[]{:S(2)}) copy-start(bf16[256,1024]{1,0:T(8,128)(2,1)S(1)} %collective-permute-done.5.refs_9_) | copy-start | bytes 1572868
  62.7 16.6 %collective-permute-start.7 = (bf16[256,1024]{1,0:T(8,128)(2,1)}, bf16[256,1024]{1,0:T(8,128)(2,1)}, u32[]{:S(2)}, u32[]{:S(2)}) collective-permute-start(bf16[256,1024]{1,0:T(8,128)(2,1)} %get-tuple-element.53), channel_id=1, source_target_pairs={{0,1},{1,0},{8,9},{9,8},{16,17},{17,16},{24,25},{25,24},{2,3},{3,2... | collective-permute-start | bytes 1572872 | tf_op jit(solution)/shard_map/ppermute | solution.py:266
  63.3 22.3 %collective-permute-start.8 = (bf16[256,1024]{1,0:T(8,128)(2,1)}, bf16[256,1024]{1,0:T(8,128)(2,1)}, u32[]{:S(2)}, u32[]{:S(2)}) collective-permute-start(bf16[256,1024]{1,0:T(8,128)(2,1)} %get-tuple-element.54), channel_id=1, source_target_pairs={{0,17},{1,16},{8,25},{9,24},{16,1},{17,0},{24,9},{25,8},{2,19},{3,... | collective-permute-start | bytes 1572872 | tf_op jit(solution)/shard_map/ppermute | solution.py:266
  68.5 34.4 %copy-start.1 = (bf16[1024,256]{1,0:T(8,128)(2,1)S(1)}, bf16[1024,256]{1,0:T(8,128)(2,1)}, u32[]{:S(2)}) copy-start(bf16[1024,256]{1,0:T(8,128)(2,1)} %mine_ref.1) | copy-start | bytes 1572868
  85.6 17.4 %all-to-all-start.2 = ((bf16[16,16,1024]{2,1,0:T(8,128)(2,1)}), bf16[16,16,1024]{2,1,0:T(8,128)(2,1)S(1)}, u32[]{:S(2)}, u32[]{:S(2)}) async-start(bf16[16,16,1024]{2,1,0:T(8,128)(2,1)} %shard_map.136), calls=%async_computation.2 | async-start | bytes 1048576 | tf_op jit(solution)/shard_map/all_to_all | solution.py:371
  89.6 53.9 %copy-start.2 = (s32[4]{0:T(128)}, s32[4]{0:T(128)S(1)}, u32[]{:S(2)}) copy-start(s32[4]{0:T(128)S(1)} %pad_add_fusion.place_ref) | copy-start | bytes 52
  103.9 8.1 %collective-permute-start.9 = (f32[16,8,512]{2,1,0:T(8,128)S(1)}, f32[16,8,512]{2,1,0:T(8,128)S(1)}, u32[]{:S(2)}, u32[]{:S(2)}) collective-permute-start(f32[16,8,512]{2,1,0:T(8,128)S(1)} %get-tuple-element.66), channel_id=1, source_target_pairs={{0,32},{32,0},{1,33},{33,1},{2,34},{34,2},{3,35},{35,3},{4,36},{36... | collective-permute-start | bytes 786440 | tf_op jit(solution)/shard_map/ppermute | solution.py:40
  110.7 6.5 %collective-permute-start.6 = (bf16[32,256]{1,0:T(8,128)(2,1)S(1)}, bf16[32,256]{1,0:T(8,128)(2,1)S(1)}, u32[]{:S(2)}, u32[]{:S(2)}) collective-permute-start(bf16[32,256]{1,0:T(8,128)(2,1)S(1)} %convolution_convert_fusion.2), channel_id=1, source_target_pairs={{0,1},{1,0},{2,3},{3,2},{4,5},{5,4},{6,7},{7,6},{8,9},{9,8},{10,11... | collective-permute-start | bytes 49160 | tf_op jit(solution)/shard_map/ppermute | solution.py:40
  112.1 5.1 %collective-permute-start.10 = (f32[32,512]{1,0:T(8,128)S(1)}, f32[32,512]{1,0:T(8,128)S(1)}, u32[]{:S(2)}, u32[]{:S(2)}) collective-permute-start(f32[32,512]{1,0:T(8,128)S(1)} %get-tuple-element.93), channel_id=1, source_target_pairs={{0,64},{64,128},{128,192},{192,0},{1,65},{65,129},{129,193},{193,1... | collective-permute-start | bytes 196616 | tf_op jit(solution)/shard_map/ppermute | solution.py:40
  113.5 5.7 %collective-permute-start.11 = (f32[32,512]{1,0:T(8,128)S(1)}, f32[32,512]{1,0:T(8,128)S(1)}, u32[]{:S(2)}, u32[]{:S(2)}) collective-permute-start(f32[32,512]{1,0:T(8,128)S(1)} %get-tuple-element.95), channel_id=1, source_target_pairs={{0,128},{64,192},{128,0},{192,64},{1,129},{65,193},{129,1},{193,65... | collective-permute-start | bytes 196616 | tf_op jit(solution)/shard_map/ppermute | solution.py:40
  116.1 3.4 %collective-permute-start.12 = (f32[32,512]{1,0:T(8,128)S(1)}, f32[32,512]{1,0:T(8,128)S(1)}, u32[]{:S(2)}, u32[]{:S(2)}) collective-permute-start(f32[32,512]{1,0:T(8,128)S(1)} %get-tuple-element.94), channel_id=1, source_target_pairs={{0,192},{64,0},{128,64},{192,128},{1,193},{65,1},{129,65},{193,129... | collective-permute-start | bytes 196616 | tf_op jit(solution)/shard_map/ppermute | solution.py:40
  119.7 37.4 %copy-start.11 = (s32[1,512]{1,0:T(1,128)S(1)}, s32[1,512]{1,0:T(1,128)}, u32[]{:S(2)}) copy-start(s32[1,512]{1,0:T(1,128)} %param.25) | copy-start | bytes 6148
  138.1 5.3 %copy-start.3 = (bf16[32,32,512]{2,1,0:T(8,128)(2,1)}, bf16[32,32,512]{2,1,0:T(8,128)(2,1)S(1)}, u32[]{:S(2)}) copy-start(bf16[32,32,512]{2,1,0:T(8,128)(2,1)S(1)} %all_to_all.25) | copy-start | bytes 3145732
  138.1 5.3 %collective-permute-start.13 = (bf16[4,256,512]{2,1,0:T(8,128)(2,1)S(1)}, bf16[4,256,512]{2,1,0:T(8,128)(2,1)S(1)}, u32[]{:S(2)}, u32[]{:S(2)}) collective-permute-start(bf16[4,256,512]{2,1,0:T(8,128)(2,1)S(1)} %bitcast.42), channel_id=1, source_target_pairs={{0,32},{32,0},{1,33},{33,1},{2,34},{34,2},{3,35},{35,3},{4,36},{36... | collective-permute-start | bytes 3145736 | tf_op jit(solution)/shard_map/ppermute | solution.py:40
  143.5 1.0 copy-start.4
  151.8 14.1 %collective-permute-start.14 = (bf16[128,1152]{1,0:T(8,128)(2,1)}, bf16[128,1152]{1,0:T(8,128)(2,1)S(1)}, u32[]{:S(2)}, u32[]{:S(2)}) collective-permute-start(bf16[128,1152]{1,0:T(8,128)(2,1)} %get-tuple-element.76), channel_id=1, source_target_pairs={{0,4},{2,6},{4,0},{6,2},{1,5},{3,7},{5,1},{7,3},{8,12},{10,14},{12... | collective-permute-start | bytes 884744 | tf_op jit(solution)/shard_map/ppermute | solution.py:40
  153.0 22.7 %collective-permute-start.15 = (bf16[128,1152]{1,0:T(8,128)(2,1)}, bf16[128,1152]{1,0:T(8,128)(2,1)S(1)}, u32[]{:S(2)}, u32[]{:S(2)}) collective-permute-start(bf16[128,1152]{1,0:T(8,128)(2,1)} %get-tuple-element.77), channel_id=1, source_target_pairs={{0,2},{2,4},{4,6},{6,0},{1,3},{3,5},{5,7},{7,1},{8,10},{10,12},{12... | collective-permute-start | bytes 884744 | tf_op jit(solution)/shard_map/ppermute | solution.py:40
  155.7 27.2 %collective-permute-start.16 = (bf16[128,1152]{1,0:T(8,128)(2,1)}, bf16[128,1152]{1,0:T(8,128)(2,1)S(1)}, u32[]{:S(2)}, u32[]{:S(2)}) collective-permute-start(bf16[128,1152]{1,0:T(8,128)(2,1)} %get-tuple-element.78), channel_id=1, source_target_pairs={{0,6},{2,0},{4,2},{6,4},{1,7},{3,1},{5,3},{7,5},{8,14},{10,8},{12,... | collective-permute-start | bytes 884744 | tf_op jit(solution)/shard_map/ppermute | solution.py:40
Sparse Core Ops, SparseCore 0:
  9.2 56.5 all-gather.2
